TPU v7x, 32 devices: a whole 2x2x4 slice. The times are simulated.
32 devices in a mesh: row: 2 (over y), col: 16 (over z, x, core).
Axes of the slice: x: 2, y: 2, z: 4, core: 2. Of those that a mesh axis runs over, the one named last changes fastest.
Arguments:
- pixels: bfloat16 [6304, 768], P('row', 'col'), may hold values from -6 to 6
- mask_places: int32 [32, 80], P('col'), may hold values from 1 to 196, as said below
- mask_count: int32 [32], P('col'), may hold values from 40 to 80, as said below
- targets: int32 [32, 80], P('col'), may hold values from 0 to 8191
- step_count: int32 [1], replicated, may hold values from 1 to 20
- patch_weight: float32 [768, 768], P('col', 'row'), may hold values from -0.21875 to 0.21875
- vector_table: float32 [205, 768], P(None, 'row')
- input_weight: float32 [1, 768, 2304], P(None, 'row', 'col'), may hold values from -0.21875 to 0.21875
- output_weight: float32 [1, 768, 768], P(None, 'col', 'row'), may hold values from -0.625 to 0.625
- upward_weight: float32 [1, 768, 3072], P(None, 'row', 'col'), may hold values from -0.21875 to 0.21875
- downward_weight: float32 [1, 3072, 768], P(None, 'col', 'row'), may hold values from -0.109375 to 0.109375
- head_weight: float32 [768, 8192], P(None, 'row'), may hold values from -0.21875 to 0.21875
- drift_patch: float32 [768, 768], P('col', 'row'), may hold values from -4.5776367e-05 to 4.5776367e-05
- drift_table: float32 [205, 768], P(None, 'row'), may hold values from -4.5776367e-05 to 4.5776367e-05
- drift_input: float32 [1, 768, 2304], P(None, 'row', 'col'), may hold values from -4.5776367e-05 to 4.5776367e-05
- drift_output: float32 [1, 768, 768], P(None, 'col', 'row'), may hold values from -4.5776367e-05 to 4.5776367e-05
- drift_upward: float32 [1, 768, 3072], P(None, 'row', 'col'), may hold values from -4.5776367e-05 to 4.5776367e-05
- drift_downward: float32 [1, 3072, 768], P(None, 'col', 'row'), may hold values from -4.5776367e-05 to 4.5776367e-05
- drift_head: float32 [768, 8192], P(None, 'row'), may hold values from -4.5776367e-05 to 4.5776367e-05
- power_patch: float32 [768, 768], P('col', 'row'), may hold values from 2.1251565e-13 to 2.1251564e-12
- power_table: float32 [205, 768], P(None, 'row'), may hold values from 2.1251565e-13 to 2.1251564e-12
- power_input: float32 [1, 768, 2304], P(None, 'row', 'col'), may hold values from 2.1251565e-13 to 2.1251564e-12
- power_output: float32 [1, 768, 768], P(None, 'col', 'row'), may hold values from 2.1251565e-13 to 2.1251564e-12
- power_upward: float32 [1, 768, 3072], P(None, 'row', 'col'), may hold values from 2.1251565e-13 to 2.1251564e-12
- power_downward: float32 [1, 3072, 768], P(None, 'col', 'row'), may hold values from 2.1251565e-13 to 2.1251564e-12
- power_head: float32 [768, 8192], P(None, 'row'), may hold values from 2.1251565e-13 to 2.1251564e-12
Outputs:
- mean_loss: float32 [], replicated
- grad_norm: float32 [], replicated
- patch_update: float32 [768, 768], P('col', 'row')
- patch_drift: float32 [768, 768], P('col', 'row')
- patch_power: float32 [768, 768], P('col', 'row')
- table_update: float32 [205, 768], P(None, 'row')
- table_drift: float32 [205, 768], P(None, 'row')
- table_power: float32 [205, 768], P(None, 'row')
- input_update: float32 [1, 768, 2304], P(None, 'row', 'col')
- input_drift: float32 [1, 768, 2304], P(None, 'row', 'col')
- input_power: float32 [1, 768, 2304], P(None, 'row', 'col')
- output_update: float32 [1, 768, 768], P(None, 'col', 'row')
- output_drift: float32 [1, 768, 768], P(None, 'col', 'row')
- output_power: float32 [1, 768, 768], P(None, 'col', 'row')
- upward_update: float32 [1, 768, 3072], P(None, 'row', 'col')
- upward_drift: float32 [1, 768, 3072], P(None, 'row', 'col')
- upward_power: float32 [1, 768, 3072], P(None, 'row', 'col')
- downward_update: float32 [1, 3072, 768], P(None, 'col', 'row')
- downward_drift: float32 [1, 3072, 768], P(None, 'col', 'row')
- downward_power: float32 [1, 3072, 768], P(None, 'col', 'row')
- head_update: float32 [768, 8192], P(None, 'row')
- head_drift: float32 [768, 8192], P(None, 'row')
- head_power: float32 [768, 8192], P(None, 'row')
Inputs may be any that keep to these rules, and one draw needn't show every extreme that they name: `mask_places`: within each image the 80 places are distinct; slot j counts when j < mask_count of that image. `mask_count`: some image has exactly 80 counted slots.
All inputs are finite; a program needn't handle non-finite values.
Results may differ from a plain program's by a relative error of at most 0.024.
Values may be sent and summed in bfloat16 or wider, within the bound.
A program may use at most 256 MiB of HBM per device.

v0:
```python
import math

import jax
import jax.numpy as jnp
from jax import lax
from jax.sharding import PartitionSpec as P

HEADS = 12
HD = 64
SEQ = 197
MSLOT = 80
LAYERS = 1


norm_eps = 1e-06
clip_limit = 0.1
learn_rate = 0.01
beta_first = 0.9
beta_second = 0.999
adam_eps = 1e-08
weight_decay = 0.05
highest = lax.Precision.HIGHEST


def combined_all(value, axis, join):
    pieces = jax.tree.map(lambda part: lax.all_gather(part, axis), value)
    head = jax.tree.map(lambda part: part[0], pieces)
    tail = jax.tree.map(lambda part: part[1:], pieces)
    so_far, _ = lax.scan(lambda so_far, section: (join(so_far, section), None), head, tail)
    return so_far


def tokens_wide(values):
    return lax.all_gather(values, "col", axis=0, tiled=True)


def tokens_tall(values):
    return lax.all_gather(values, "row", axis=0, tiled=True)


def row_total(partial_sum):
    return lax.psum_scatter(partial_sum, "row", scatter_dimension=0, tiled=True)


def col_total(partial_sum):
    return lax.psum_scatter(partial_sum, "col", scatter_dimension=0, tiled=True)


def image_swap(values):
    return lax.all_to_all(values, "col", split_axis=0, concat_axis=0, tiled=True)


def to_images(values):
    col_count = lax.axis_size("col")
    height, breadth = values.shape
    received = image_swap(values.reshape(col_count, height // col_count, breadth))
    return jnp.moveaxis(received, 0, 1).reshape(height // col_count, col_count * breadth)


def from_images(values):
    col_count = lax.axis_size("col")
    height, breadth = values.shape
    sent = jnp.moveaxis(values.reshape(height, col_count, breadth // col_count), 1, 0)
    return image_swap(sent).reshape(col_count * height, breadth // col_count)


def feature_total(first_sum, second_sum):
    return lax.psum((first_sum, second_sum), "row")


def norm_forward(values, gain, shift):
    width = gain.shape[0] * lax.axis_size("row")
    summed, squared = feature_total(jnp.sum(values, axis=1), jnp.sum(values * values, axis=1))
    center = summed / width
    spread = squared / width - center * center
    inverse = lax.rsqrt(spread + norm_eps)
    scaled = (values - center[:, None]) * inverse[:, None]
    return (scaled * gain + shift, (scaled, inverse))


def norm_backward(upstream, kept, gain):
    scaled, inverse = kept
    width = gain.shape[0] * lax.axis_size("row")
    inner = upstream * gain
    summed, crossed = feature_total(jnp.sum(inner, axis=1), jnp.sum(inner * scaled, axis=1))
    downstream = inverse[:, None] * (
        inner - summed[:, None] / width - scaled * (crossed[:, None] / width)
    )
    return (downstream, jnp.sum(upstream * scaled, axis=0), jnp.sum(upstream, axis=0))


def exact_gelu(values):
    return jax.nn.gelu(values, approximate=False)


def split_heads(grouped):
    images = grouped.shape[0] // SEQ
    pieces = grouped.reshape(images, SEQ, 3, HEADS, HD)
    return (pieces[:, :, 0], pieces[:, :, 1], pieces[:, :, 2])


def attention_weights(query, keys):
    scores = jnp.einsum("iqhd,ikhd->ihqk", query, keys, preferred_element_type=jnp.float32)
    return jax.nn.softmax(scores * (1.0 / math.sqrt(HD)), axis=-1)


def attend(grouped):
    query, keys, values = split_heads(grouped)
    weights_low = attention_weights(query, keys).astype(jnp.bfloat16)
    mixture = jnp.einsum("ihqk,ikhd->iqhd", weights_low, values, preferred_element_type=jnp.float32)
    return mixture.reshape(grouped.shape[0], HEADS * HD)


def attend_back(grouped, grad_mixture):
    query, keys, values = split_heads(grouped)
    images = query.shape[0]
    weights_full = attention_weights(query, keys)
    weights_low = weights_full.astype(jnp.bfloat16)
    grad_out = grad_mixture.reshape(images, SEQ, HEADS, HD)
    grad_weights = jnp.einsum(
        "iqhd,ikhd->ihqk", grad_out, values, preferred_element_type=jnp.float32
    )
    grad_values = jnp.einsum(
        "ihqk,iqhd->ikhd", weights_low, grad_out, preferred_element_type=jnp.float32
    )
    centered = grad_weights - jnp.sum(weights_full * grad_weights, axis=-1, keepdims=True)
    grad_scores = (weights_full * centered).astype(jnp.bfloat16)
    scale = 1.0 / math.sqrt(HD)
    grad_query = (
        jnp.einsum("ihqk,ikhd->iqhd", grad_scores, keys, preferred_element_type=jnp.float32) * scale
    )
    grad_keys = (
        jnp.einsum("ihqk,iqhd->ikhd", grad_scores, query, preferred_element_type=jnp.float32)
        * scale
    )
    stacked = jnp.stack([grad_query, grad_keys, grad_values], axis=2)
    return stacked.reshape(images * SEQ, 3 * HEADS * HD)


def layer_forward(stream, weights, gains):
    input_low, output_low, upward_low, downward_low = weights
    normed_one, stats_one = norm_forward(stream, gains[0], gains[1])
    wide_one = tokens_wide(normed_one.astype(jnp.bfloat16))
    projected = row_total(jnp.dot(wide_one, input_low, preferred_element_type=jnp.float32))
    grouped = to_images(projected.astype(jnp.bfloat16))
    mixture = attend(grouped)
    spread_tall = tokens_tall(from_images(mixture.astype(jnp.bfloat16)))
    stream_mid = stream + col_total(
        jnp.dot(spread_tall, output_low, preferred_element_type=jnp.float32)
    )
    normed_two, stats_two = norm_forward(stream_mid, gains[2], gains[3])
    wide_two = tokens_wide(normed_two.astype(jnp.bfloat16))
    hidden_pre = row_total(jnp.dot(wide_two, upward_low, preferred_element_type=jnp.float32))
    hidden_act = tokens_tall(exact_gelu(hidden_pre).astype(jnp.bfloat16))
    stream_out = stream_mid + col_total(
        jnp.dot(hidden_act, downward_low, preferred_element_type=jnp.float32)
    )
    return (
        stream_out,
        (stats_one, wide_one, grouped, spread_tall, stats_two, wide_two, hidden_pre, hidden_act),
    )


def layer_backward(grad_stream, saved, weights, gains):
    stats_one, wide_one, grouped, spread_tall, stats_two, wide_two, hidden_pre, hidden_act = saved
    input_low, output_low, upward_low, downward_low = weights
    grad_two_wide = tokens_wide(grad_stream.astype(jnp.bfloat16))
    grad_downward = jnp.einsum(
        "tf,td->fd", hidden_act, grad_two_wide, preferred_element_type=jnp.float32
    )
    grad_act = row_total(
        jnp.einsum("td,fd->tf", grad_two_wide, downward_low, preferred_element_type=jnp.float32)
    )
    gelu_value, gelu_pull = jax.vjp(exact_gelu, hidden_pre)
    grad_pre = tokens_tall(gelu_pull(grad_act)[0].astype(jnp.bfloat16))
    grad_upward = jnp.einsum("td,tf->df", wide_two, grad_pre, preferred_element_type=jnp.float32)
    grad_normed_two = col_total(
        jnp.einsum("tf,df->td", grad_pre, upward_low, preferred_element_type=jnp.float32)
    )
    grad_mid, grad_gain_two, grad_shift_two = norm_backward(grad_normed_two, stats_two, gains[2])
    grad_mid = grad_mid + grad_stream
    grad_one_wide = tokens_wide(grad_mid.astype(jnp.bfloat16))
    grad_output = jnp.einsum(
        "tc,td->cd", spread_tall, grad_one_wide, preferred_element_type=jnp.float32
    )
    grad_spread = row_total(
        jnp.einsum("td,cd->tc", grad_one_wide, output_low, preferred_element_type=jnp.float32)
    )
    grad_mixture = to_images(grad_spread.astype(jnp.bfloat16))
    grad_grouped = from_images(attend_back(grouped, grad_mixture).astype(jnp.bfloat16))
    grad_packed_tall = tokens_tall(grad_grouped)
    grad_input = jnp.einsum(
        "td,tq->dq", wide_one, grad_packed_tall, preferred_element_type=jnp.float32
    )
    grad_normed_one = col_total(
        jnp.einsum("tq,dq->td", grad_packed_tall, input_low, preferred_element_type=jnp.float32)
    )
    grad_below, grad_gain_one, grad_shift_one = norm_backward(grad_normed_one, stats_one, gains[0])
    return (
        grad_below + grad_mid,
        (grad_input, grad_output, grad_upward, grad_downward),
        (grad_gain_one, grad_shift_one, grad_gain_two, grad_shift_two),
    )


def adam_step(weight, grad, drift, power, factor, step_value):
    scaled = grad * factor
    new_drift = beta_first * drift + (1.0 - beta_first) * scaled
    new_power = beta_second * power + (1.0 - beta_second) * scaled * scaled
    drift_hat = new_drift / (1.0 - jnp.power(beta_first, step_value))
    power_hat = new_power / (1.0 - jnp.power(beta_second, step_value))
    update = -learn_rate * (drift_hat / (jnp.sqrt(power_hat) + adam_eps) + weight_decay * weight)
    return (update, new_drift, new_power)


def on_device(
    pixels,
    mask_places,
    mask_count,
    targets,
    step_count,
    patch_weight,
    vector_table,
    input_weight,
    output_weight,
    upward_weight,
    downward_weight,
    head_weight,
    drift_patch,
    drift_table,
    drift_input,
    drift_output,
    drift_upward,
    drift_downward,
    drift_head,
    power_patch,
    power_table,
    power_input,
    power_output,
    power_upward,
    power_downward,
    power_head,
):
    images = mask_places.shape[0]
    row_index = lax.axis_index("row")
    col_index = lax.axis_index("col")
    patch_low = patch_weight.astype(jnp.bfloat16)
    input_stack = input_weight.astype(jnp.bfloat16)
    output_stack = output_weight.astype(jnp.bfloat16)
    upward_stack = upward_weight.astype(jnp.bfloat16)
    downward_stack = downward_weight.astype(jnp.bfloat16)
    layer_weights = [(input_stack[0], output_stack[0], upward_stack[0], downward_stack[0])]

    def gains_of(norm_index):
        return (vector_table[SEQ + 2 + 2 * norm_index], vector_table[SEQ + 3 + 2 * norm_index])

    pixel_tall = tokens_tall(pixels)
    patch_proj = col_total(jnp.dot(pixel_tall, patch_low, preferred_element_type=jnp.float32))
    places = jnp.arange(SEQ, dtype=jnp.int32)
    counted = jnp.arange(MSLOT, dtype=jnp.int32)[None, :] < mask_count[:, None]
    matches = mask_places[:, :, None] == places[None, None, :]
    masked = jnp.any(matches & counted[:, :, None], axis=1)[:, :, None]
    opening = (places == 0)[None, :, None]
    stream = jnp.where(
        opening,
        vector_table[SEQ],
        jnp.where(masked, vector_table[SEQ + 1], patch_proj.reshape(images, SEQ, -1)),
    )
    stream = (stream + vector_table[:SEQ][None]).reshape(images * SEQ, -1)
    inputs_kept = []
    level = 0
    norms_here = gains_of(2 * level) + gains_of(2 * level + 1)
    inputs_kept.append(stream)
    stream, saved = layer_forward(stream, layer_weights[level], norms_here)
    records = [saved]
    final_gain, final_shift = gains_of(2 * LAYERS)
    final_out, final_stats = norm_forward(stream, final_gain, final_shift)
    selector = matches.astype(jnp.float32)
    picked = jnp.einsum(
        "ims,isd->imd", selector, final_out.reshape(images, SEQ, -1), precision=highest
    )
    picked_wide = lax.all_gather(
        picked.reshape(images * MSLOT, -1).astype(jnp.bfloat16), "row", axis=1, tiled=True
    )
    head_low = head_weight.astype(jnp.bfloat16)
    logits = jnp.dot(picked_wide, head_low, preferred_element_type=jnp.float32)
    vocab_local = head_weight.shape[1]
    target_local = targets.reshape(-1) - row_index * vocab_local
    target_hits = (
        target_local[:, None] == jnp.arange(vocab_local, dtype=jnp.int32)[None, :]
    ).astype(jnp.float32)
    chosen = jnp.sum(target_hits * logits, axis=1)
    local_top = jnp.max(logits, axis=1)

    def combine(left, right):
        joined = jnp.maximum(left[0], right[0])
        return (joined, left[1] * jnp.exp(left[0] - joined) + right[1] * jnp.exp(right[0] - joined))

    local_sum = jnp.sum(jnp.exp(logits - local_top[:, None]), axis=1)
    top_value, exp_total = combined_all((local_top, local_sum), "row", combine)
    log_total = top_value + jnp.log(exp_total)
    slot_weight = counted.reshape(-1).astype(jnp.float32)
    leader_row = (row_index == 0).astype(jnp.float32)
    loss_part = jnp.sum(log_total * slot_weight) * leader_row - jnp.sum(chosen * slot_weight)
    count_part = jnp.sum(mask_count.astype(jnp.float32)) * leader_row
    grad_logits = (
        (jnp.exp(logits - log_total[:, None]) - target_hits) * slot_weight[:, None]
    ).astype(jnp.bfloat16)
    grad_head_local = jnp.einsum(
        "rd,rv->dv", picked_wide, grad_logits, preferred_element_type=jnp.float32
    )
    grad_picked = lax.psum_scatter(
        jnp.einsum("rv,dv->rd", grad_logits, head_low, preferred_element_type=jnp.float32).astype(
            jnp.bfloat16
        ),
        "row",
        scatter_dimension=1,
        tiled=True,
    ).astype(jnp.float32)
    grad_final = jnp.einsum(
        "ims,imd->isd", selector, grad_picked.reshape(images, MSLOT, -1), precision=highest
    )
    grad_stream, grad_final_gain, grad_final_shift = norm_backward(
        grad_final.reshape(images * SEQ, -1), final_stats, final_gain
    )
    weight_grads = [None] * LAYERS
    norm_grads = [None] * LAYERS
    for level in reversed(range(LAYERS)):
        norms_here = gains_of(2 * level) + gains_of(2 * level + 1)
        saved = records[level]
        grad_stream, weight_grads[level], norm_grads[level] = layer_backward(
            grad_stream, saved, layer_weights[level], norms_here
        )
    layer_lines = jnp.stack([line for level in range(LAYERS) for line in norm_grads[level]])
    grad_input = jnp.stack([weight_grads[0][0]])
    grad_output = jnp.stack([weight_grads[0][1]])
    grad_upward = jnp.stack([weight_grads[0][2]])
    grad_downward = jnp.stack([weight_grads[0][3]])
    grad_grid = grad_stream.reshape(images, SEQ, -1)
    grad_patch = jnp.where(opening | masked, 0.0, grad_grid).reshape(images * SEQ, -1)
    grad_patch_wide = tokens_wide(grad_patch.astype(jnp.bfloat16))
    grad_patch_weight = jnp.einsum(
        "tp,td->pd", pixel_tall, grad_patch_wide, preferred_element_type=jnp.float32
    )
    table_local = jnp.concatenate(
        [
            jnp.sum(grad_grid, axis=0),
            jnp.sum(grad_grid[:, 0], axis=0)[None],
            jnp.sum(jnp.where(masked, grad_grid, 0.0), axis=(0, 1))[None],
            layer_lines,
            jnp.stack([grad_final_gain, grad_final_shift]),
        ],
        axis=0,
    )
    grad_table, grad_head = (
        lax.psum(table_local.astype(jnp.bfloat16), "col").astype(jnp.float32),
        lax.psum(grad_head_local.astype(jnp.bfloat16), "col").astype(jnp.float32),
    )
    leader_col = (col_index == 0).astype(jnp.float32)
    squares_part = (
        jnp.sum(grad_patch_weight * grad_patch_weight)
        + jnp.sum(grad_input * grad_input)
        + jnp.sum(grad_output * grad_output)
        + jnp.sum(grad_upward * grad_upward)
        + jnp.sum(grad_downward * grad_downward)
        + leader_col * (jnp.sum(grad_table * grad_table) + jnp.sum(grad_head * grad_head))
    )
    loss_total, count_total, squares_total = lax.psum(
        (loss_part, count_part, squares_part), ("row", "col")
    )
    mean_loss = loss_total / count_total
    grad_norm = jnp.sqrt(squares_total) / count_total
    factor = jnp.minimum(1.0, clip_limit / grad_norm) / count_total
    step_value = step_count[0].astype(jnp.float32)
    patch_result = adam_step(
        patch_weight, grad_patch_weight, drift_patch, power_patch, factor, step_value
    )
    table_result = adam_step(vector_table, grad_table, drift_table, power_table, factor, step_value)
    input_result = adam_step(input_weight, grad_input, drift_input, power_input, factor, step_value)
    output_result = adam_step(
        output_weight, grad_output, drift_output, power_output, factor, step_value
    )
    upward_result = adam_step(
        upward_weight, grad_upward, drift_upward, power_upward, factor, step_value
    )
    downward_result = adam_step(
        downward_weight, grad_downward, drift_downward, power_downward, factor, step_value
    )
    head_result = adam_step(head_weight, grad_head, drift_head, power_head, factor, step_value)
    return (
        mean_loss,
        grad_norm,
        patch_result[0],
        patch_result[1],
        patch_result[2],
        table_result[0],
        table_result[1],
        table_result[2],
        input_result[0],
        input_result[1],
        input_result[2],
        output_result[0],
        output_result[1],
        output_result[2],
        upward_result[0],
        upward_result[1],
        upward_result[2],
        downward_result[0],
        downward_result[1],
        downward_result[2],
        head_result[0],
        head_result[1],
        head_result[2],
    )


def solution(mesh):
    return jax.shard_map(
        on_device,
        mesh=mesh,
        in_specs=(
            P("row", "col"),
            P("col", None),
            P("col"),
            P("col", None),
            P(),
            P("col", "row"),
            P(None, "row"),
            P(None, "row", "col"),
            P(None, "col", "row"),
            P(None, "row", "col"),
            P(None, "col", "row"),
            P(None, "row"),
            P("col", "row"),
            P(None, "row"),
            P(None, "row", "col"),
            P(None, "col", "row"),
            P(None, "row", "col"),
            P(None, "col", "row"),
            P(None, "row"),
            P("col", "row"),
            P(None, "row"),
            P(None, "row", "col"),
            P(None, "col", "row"),
            P(None, "row", "col"),
            P(None, "col", "row"),
            P(None, "row"),
        ),
        out_specs=(
            P(),
            P(),
            P("col", "row"),
            P("col", "row"),
            P("col", "row"),
            P(None, "row"),
            P(None, "row"),
            P(None, "row"),
            P(None, "row", "col"),
            P(None, "row", "col"),
            P(None, "row", "col"),
            P(None, "col", "row"),
            P(None, "col", "row"),
            P(None, "col", "row"),
            P(None, "row", "col"),
            P(None, "row", "col"),
            P(None, "row", "col"),
            P(None, "col", "row"),
            P(None, "col", "row"),
            P(None, "col", "row"),
            P(None, "row"),
            P(None, "row"),
            P(None, "row"),
        ),
        check_vma=False,
    )
```

profile of v0, /device:TPU:0, one launch (start us, length us, event | category | flops | bytes accessed | tf_op | source)
XLA Modules:
  0.0 1870.7 jit_solution(75962706965788246)
XLA Ops:
  7.2 11.2 all-gather.2
  24.7 103.8 %fusion = f32[400,384]{1,0:T(8,128)S(1)} fusion(f32[6304,384]{1,0:T(8,128)} %fusion.84), kind=kCustom, calls=%all-reduce-scatter | all-reduce-scatter fusion | flops 2457601 | bytes 10297856
  128.5 7.3 collective-permute-start
  144.5 58.4 %all-gather.21.cloned.1.call-done = bf16[16,394,384]{2,1,0:T(8,128)(2,1)} async-done(((bf16[1,394,384]{2,1,0:T(8,128)(2,1)}), bf16[16,394,384]{2,1,0:T(8,128)(2,1)}) %all-gather.21.cloned.1.call-update) | async-done | bytes 4841488 | tf_op jit(solution)/shard_map/all_gather | solution.py:34
  215.5 77.5 %reduce-scatter.26.cloned.1.call-done = f32[3152,144]{1,0:T(8,128)} async-done(((f32[6304,144]{1,0:T(8,128)}), f32[3152,144]{1,0:T(8,128)}) %reduce-scatter.26.cloned.1.call-update) | async-done | bytes 1815568
  299.2 34.9 %all_to_all.20 = bf16[16,197,144]{1,2,0:T(8,128)(2,1)S(1)} all-to-all(bf16[16,197,144]{1,2,0:T(8,128)(2,1)S(1)} %copy.80), channel_id=1, replica_groups=mesh['row'=2,'col'=16] {'col'}, dimensions={0} | all-to-all | bytes 1815552 | tf_op jit(solution)/shard_map/all_to_all | solution.py:50
  338.2 15.3 all_to_all.21
  354.1 10.3 all-gather.4
  370.6 103.8 %fusion.1 = f32[400,384]{1,0:T(8,128)S(1)} fusion(f32[6304,384]{1,0:T(8,128)} %fusion.82), kind=kCustom, calls=%all-reduce-scatter.1 | all-reduce-scatter fusion | flops 2457601 | bytes 10297856
  488.3 56.9 %all-gather.23.cloned.1.call-done = bf16[16,394,384]{2,1,0:T(8,128)(2,1)} async-done(((bf16[1,394,384]{2,1,0:T(8,128)(2,1)}), bf16[16,394,384]{2,1,0:T(8,128)(2,1)}) %all-gather.23.cloned.1.call-update) | async-done | bytes 4841488 | tf_op jit(solution)/shard_map/all_gather | solution.py:34
  557.8 77.5 %reduce-scatter.28.cloned.1.call-done = f32[3152,192]{1,0:T(8,128)} async-done(((f32[6304,192]{1,0:T(8,128)}), f32[3152,192]{1,0:T(8,128)}) %reduce-scatter.28.cloned.1.call-update) | async-done | bytes 2420752
  645.0 36.7 %all-gather.25.cloned.1.call-done = bf16[2,3152,192]{1,2,0:T(8,128)(2,1)} async-done(((bf16[1,3152,192]{1,2,0:T(8,128)(2,1)}), bf16[2,3152,192]{1,2,0:T(8,128)(2,1)}) %all-gather.25.cloned.1.call-update) | async-done | bytes 2420752 | tf_op jit(solution)/shard_map/all_gather | solution.py:38
  698.1 104.2 %fusion.2 = f32[400,384]{1,0:T(8,128)S(1)} fusion(f32[6304,384]{1,0:T(8,128)} %fusion.58), kind=kCustom, calls=%all-reduce-scatter.2 | all-reduce-scatter fusion | flops 2457601 | bytes 10297856
  835.9 7.7 fusion.31
  845.7 16.7 reduce-scatter.30.cloned.1.call-done
  878.3 54.6 %all-gather.27.cloned.1.call-done = bf16[16,394,384]{2,1,0:T(8,128)(2,1)} async-done(((bf16[1,394,384]{2,1,0:T(8,128)(2,1)}), bf16[16,394,384]{2,1,0:T(8,128)(2,1)}) %all-gather.27.cloned.1.call-update) | async-done | bytes 4841488 | tf_op jit(solution)/shard_map/all_gather | solution.py:34
  945.6 77.5 %reduce-scatter.32.cloned.1.call-done = f32[3152,192]{1,0:T(8,128)} async-done(((f32[6304,192]{1,0:T(8,128)}), f32[3152,192]{1,0:T(8,128)}) %reduce-scatter.32.cloned.1.call-update) | async-done | bytes 2420752
  1031.8 37.3 %all-gather.29.cloned.1.call-done = bf16[2,3152,192]{1,2,0:T(8,128)(2,1)} async-done(((bf16[1,3152,192]{1,2,0:T(8,128)(2,1)}), bf16[2,3152,192]{1,2,0:T(8,128)(2,1)}) %all-gather.29.cloned.1.call-update) | async-done | bytes 2420752 | tf_op jit(solution)/shard_map/all_gather | solution.py:38
  1079.6 7.4 fusion.60
  1087.0 104.8 %fusion.3 = f32[400,384]{1,0:T(8,128)} fusion(f32[6304,384]{1,0:T(8,128)} %fusion.60), kind=kCustom, calls=%all-reduce-scatter.3 | all-reduce-scatter fusion | flops 2457601 | bytes 10297856
  1214.9 58.6 %all-gather.31.cloned.1.call-done = bf16[16,394,384]{2,1,0:T(8,128)(2,1)} async-done(((bf16[1,394,384]{2,1,0:T(8,128)(2,1)}), bf16[16,394,384]{2,1,0:T(8,128)(2,1)}) %all-gather.31.cloned.1.call-update) | async-done | bytes 4841488 | tf_op jit(solution)/shard_map/all_gather | solution.py:34
  1284.5 42.9 %reduce-scatter.34.cloned.1.call-done = f32[3152,48]{1,0:T(8,128)} async-done(((f32[6304,48]{1,0:T(8,128)}), f32[3152,48]{1,0:T(8,128)}) %reduce-scatter.34.cloned.1.call-update) | async-done | bytes 605200
  1333.9 17.6 all_to_all.22
  1357.0 32.8 %all_to_all.23 = bf16[16,197,144]{1,2,0:T(8,128)(2,1)S(1)} all-to-all(bf16[16,197,144]{1,2,0:T(8,128)(2,1)S(1)} %bitcast.204), channel_id=1, replica_groups=mesh['row'=2,'col'=16] {'col'}, dimensions={0} | all-to-all | bytes 1815552 | tf_op jit(solution)/shard_map/all_to_all | solution.py:50
  1394.9 28.0 %all-gather.33.cloned.1.call-done = bf16[2,3152,144]{1,2,0:T(8,128)(2,1)} async-done(((bf16[1,3152,144]{1,2,0:T(8,128)(2,1)}), bf16[2,3152,144]{1,2,0:T(8,128)(2,1)}) %all-gather.33.cloned.1.call-update) | async-done | bytes 1815568 | tf_op jit(solution)/shard_map/all_gather | solution.py:38
  1431.2 7.2 fusion.64
  1438.5 104.8 %fusion.4 = f32[400,384]{1,0:T(8,128)} fusion(f32[6304,384]{1,0:T(8,128)} %fusion.64), kind=kCustom, calls=%all-reduce-scatter.4 | all-reduce-scatter fusion | flops 2457601 | bytes 10297856
  1544.2 7.7 collective-permute-start.4
  1589.2 123.3 %all-reduce.23.cloned.1.call-done = (bf16[205,384]{1,0:T(8,128)(2,1)}, bf16[768,4096]{1,0:T(8,128)(2,1)}) async-done(((bf16[205,384]{1,0:T(8,128)(2,1)}, bf16[768,4096]{1,0:T(8,128)(2,1)}), (bf16[205,384]{1,0:T(8,128)(2,1)}, bf16[768,4096]{1,0:T(8,128)(2,1)})) %all-reduce.23.cloned.1.call-update) | async-done | bytes 6448912 | tf_op jit(solution)/shard_map/psum | solution.py:356
  1722.1 47.5 %all-gather.35.cloned.1.call-done = bf16[16,394,384]{2,1,0:T(8,128)(2,1)} async-done(((bf16[1,394,384]{2,1,0:T(8,128)(2,1)}), bf16[16,394,384]{2,1,0:T(8,128)(2,1)}) %all-gather.35.cloned.1.call-update) | async-done | bytes 4841488 | tf_op jit(solution)/shard_map/all_gather | solution.py:34
  1782.8 39.4 %all-reduce.12 = (f32[]{:T(128)}, f32[]{:T(128)}, f32[]{:T(128)}) all-reduce(f32[]{:T(128)S(6)} %sub.189, f32[]{:T(128)S(6)} %mul.675, f32[]{:T(128)S(6)} %add.292), channel_id=1, replica_groups=mesh['row'=2,'col'=16] {'row','col'}, use_global_device_ids=true, to_apply=%region_25.26 | all-reduce | flops 3 | bytes 24 | tf_op jit(solution)/shard_map/psum | solution.py:368
  1826.4 29.7 %add_multiply_fusion = (f32[768,4096]{1,0:T(8,128)}, f32[768,4096]{1,0:T(8,128)}, f32[768,4096]{1,0:T(8,128)}) fusion(f32[768,4096]{1,0:T(8,128)} %param.37, f32[]{:T(128)} %bitcast.45, f32[]{:T(128)} %bitcast.44, f32[]{:T(128)S(6)} %div.169, bf16[768,4096]{1,0:T(8,128)(2,1)} %get-tuple-element.84, f32[768,4096]{1,0:T(8,128)} %param.51, f32[768,4096]{1,0:T(8,128)} %param.44), kind=kLoop, calls=%fused_computation.8 | loop fusion | flops 50331648 | bytes 81788944 | tf_op jit(solution)/shard_map/mul | solution.py:212
  (352 shorter events, 297.4 us)
Async XLA Ops:
  7.2 195.7 %all-gather.21.cloned.1.call-start = ((), (), s32[]{:S(2)}) async-start(), calls=%async_computation.9 | async-start | bytes 5222400 | tf_op jit(solution)/shard_map/all_gather | solution.py:34
  24.7 111.1 %copy-start.74 = (s32[2]{0:T(128)S(1)}, s32[2]{0:T(128)}, u32[]{:S(2)}) copy-start(s32[2]{0:T(128)} %param.28) | copy-start | bytes 28
  24.7 111.2 %copy-start.55 = (s32[2,80]{1,0:T(2,128)S(1)}, s32[2,80]{1,0:T(2,128)}, u32[]{:S(2)}) copy-start(s32[2,80]{1,0:T(2,128)} %param.27) | copy-start | bytes 1924
  24.7 111.6 %slice-start.4 = ((f32[205,384]{1,0:T(8,128)}), f32[197,384]{1,0:T(8,128)S(1)}, s32[]{:S(2)}) async-start(f32[205,384]{1,0:T(8,128)} %param.32), calls=%async_computation.27 | async-start | bytes 614400 | tf_op jit(solution)/shard_map/slice | solution.py:269
  128.5 9.2 collective-permute-start
  135.9 509.0 %copy-start.69 = (pred[2,80]{1,0:T(4,128)(4,1)}, pred[2,80]{1,0:T(4,128)(4,1)S(1)}, u32[]{:S(2)}) copy-start(pred[2,80]{1,0:T(4,128)(4,1)S(1)} %iota_compare_fusion.5) | copy-start | bytes 484
  137.7 70.8 %copy-start.47 = (f32[384]{0:T(512)}, f32[384]{0:T(512)S(1)}, u32[]{:S(2)}) copy-start(f32[384]{0:T(512)S(1)} %get-tuple-element.62) | copy-start | bytes 4612
  143.5 65.0 %copy-start.49 = (f32[394]{0:T(512)}, f32[394]{0:T(512)S(1)}, u32[]{:S(2)}) copy-start(f32[394]{0:T(512)S(1)} %get-tuple-element.126) | copy-start | bytes 4732
  143.5 65.0 %copy-start.51 = (f32[394]{0:T(512)}, f32[394]{0:T(512)S(1)}, u32[]{:S(2)}) copy-start(f32[394]{0:T(512)S(1)} %get-tuple-element.127) | copy-start | bytes 4732
  144.5 148.6 %reduce-scatter.26.cloned.1.call-start = ((), (), s32[]{:S(2)}) async-start(), calls=%async_computation.17 | async-start | bytes 9682944
  215.5 329.7 %all-gather.23.cloned.1.call-start = ((), (), s32[]{:S(2)}) async-start(), calls=%async_computation.10 | async-start | bytes 5222400 | tf_op jit(solution)/shard_map/all_gather | solution.py:34
  474.4 7.2 collective-permute-start.1
  482.3 68.4 %copy-start.2 = (f32[394,384]{1,0:T(8,128)}, f32[394,384]{1,0:T(8,128)S(1)}, u32[]{:S(2)}) copy-start(f32[394,384]{1,0:T(8,128)S(1)} %get-tuple-element.115) | copy-start | bytes 1815556
  488.2 147.1 %reduce-scatter.28.cloned.1.call-start = ((), (), s32[]{:S(2)}) async-start(), calls=%async_computation.18 | async-start | bytes 9682944
  557.7 123.9 %all-gather.25.cloned.1.call-start = ((), (), s32[]{:S(2)}) async-start(), calls=%async_computation.11 | async-start | bytes 3686400 | tf_op jit(solution)/shard_map/all_gather | solution.py:38
  644.3 218.0 %reduce-scatter.30.cloned.1.call-start = ((), (), s32[]{:S(2)}) async-start(), calls=%async_computation.19 | async-start | bytes 589824
  645.0 164.0 %copy-start.72 = (pred[160]{0:T(512)(128)(4,1)}, pred[160]{0:T(512)(128)(4,1)S(1)}, u32[]{:S(2)}) copy-start(pred[160]{0:T(512)(128)(4,1)S(1)} %lt.43) | copy-start | bytes 484
  698.1 110.8 %copy-start.68 = (s32[2,80]{1,0:T(2,128)S(1)}, s32[2,80]{1,0:T(2,128)}, u32[]{:S(2)}) copy-start(s32[2,80]{1,0:T(2,128)} %param.29) | copy-start | bytes 1924
  698.1 110.9 %copy-start.78 = (u32[32]{0:T(128)S(1)}, u32[32]{0:T(128)}, u32[]{:S(2)}) copy-start(u32[32]{0:T(128)} %constant.35) | copy-start | bytes 388
  698.1 112.6 %copy-start.3 = (f32[394,384]{1,0:T(8,128)S(1)}, f32[394,384]{1,0:T(8,128)}, u32[]{:S(2)}) copy-start(f32[394,384]{1,0:T(8,128)} %copy-done.2) | copy-start | bytes 1815556
  802.4 7.9 collective-permute-start.2
  845.5 87.5 %all-gather.27.cloned.1.call-start = ((), (), s32[]{:S(2)}) async-start(), calls=%async_computation.12 | async-start | bytes 5222400 | tf_op jit(solution)/shard_map/all_gather | solution.py:34
  878.3 144.8 %reduce-scatter.32.cloned.1.call-start = ((), (), s32[]{:S(2)}) async-start(), calls=%async_computation.20 | async-start | bytes 9682944
  945.5 123.6 %all-gather.29.cloned.1.call-start = ((), (), s32[]{:S(2)}) async-start(), calls=%async_computation.13 | async-start | bytes 3686400 | tf_op jit(solution)/shard_map/all_gather | solution.py:38
  1031.8 241.7 %all-gather.31.cloned.1.call-start = ((), (), s32[]{:S(2)}) async-start(), calls=%async_computation.14 | async-start | bytes 5222400 | tf_op jit(solution)/shard_map/all_gather | solution.py:34
  1192.7 7.6 collective-permute-start.3
  1214.6 64.4 %copy-start.28 = (f32[1,48,384]{2,1,0:T(8,128)S(1)}, f32[1,48,384]{2,1,0:T(8,128)}, u32[]{:S(2)}) copy-start(f32[1,48,384]{2,1,0:T(8,128)} %param.34) | copy-start | bytes 221188
  1214.6 112.8 %reduce-scatter.34.cloned.1.call-start = ((), (), s32[]{:S(2)}) async-start(), calls=%async_computation.21 | async-start | bytes 4841472
  1284.5 138.5 %all-gather.33.cloned.1.call-start = ((), (), s32[]{:S(2)}) async-start(), calls=%async_computation.15 | async-start | bytes 2764800 | tf_op jit(solution)/shard_map/all_gather | solution.py:38
  1394.8 317.7 %all-reduce.23.cloned.1.call-start = ((), (), s32[]{:S(2)}) async-start(), calls=%async_computation.22 | async-start | bytes 12902400 | tf_op jit(solution)/shard_map/psum | solution.py:356
  1544.2 13.2 collective-permute-start.4
  1570.1 199.5 %all-gather.35.cloned.1.call-start = ((), (), s32[]{:S(2)}) async-start(), calls=%async_computation.16 | async-start | bytes 5222400 | tf_op jit(solution)/shard_map/all_gather | solution.py:34
  (71 other events, 753.6 us)
Sparse Core Ops, SparseCore 0:
  144.6 58.3 all-gather.20
  215.6 77.3 reduce-scatter.25
  488.3 56.8 all-gather.22
  557.9 77.3 reduce-scatter.27
  644.4 37.1 all-gather.24
  845.6 16.7 reduce-scatter.29
  878.4 54.4 all-gather.26
  945.6 77.3 reduce-scatter.31
  1031.9 37.1 all-gather.28
  1214.7 58.6 all-gather.30
  1284.6 42.7 reduce-scatter.33
  1395.0 27.9 all-gather.32
  1570.2 142.3 all-reduce.22
  1715.1 54.3 all-gather.34
where the time goes:
time: 1880 us; the launch traced here: 1870 us
  waiting for transfers between devices  795 us (42%)
  blocking collectives  723 us (38%)
  local copies, waits for them, and re-layouts  108 us (6%)
  matrix products  101 us (5%)
  other arithmetic  76.7 us (4%)
  starting transfers between devices  36.3 us (2%)
  between operations  30.2 us (2%)
    unnamed x6, blocking collectives  526 us
    unnamed x24, waiting for transfers between devices  294 us
    all_gather x5, waiting for transfers between devices, tokens_wide(): return lax.all_gather(values, 'col', axis=0, tiled=True)  276 us
    psum x1, waiting for transfers between devices, on_device(): lax.psum(table_local.astype(jnp.bfloat16), 'col').astype(jnp.float32)  123 us
    all_gather x3, waiting for transfers between devices, tokens_tall(): return lax.all_gather(values, 'row', axis=0, tiled=True)  102 us
    all_to_all x4, blocking collectives, image_swap(): lax.all_to_all(values, 'col', split_axis=0, concat_axis=0, tiled=True)  101 us
    unnamed x200, local copies, waits for them, and re-layouts  76.5 us
    psum x1, blocking collectives, on_device(): lax.psum((loss_part, count_part, squares_part), ('row', 'col'))  39.4 us
  transfers between devices with their start and end apart: 19, of which 16 were waited for; matrix products, arithmetic and copies ran while one was open for 2% of the time, Pallas kernels for 0%

commit v1 on v0

v1 whole, which is shorter than its diff:
```python
import math

import jax
import jax.numpy as jnp
from jax import lax
from jax.sharding import PartitionSpec as P

HEADS = 12
HD = 64
SEQ = 197
MSLOT = 80
BOTH = ("row", "col")

norm_eps = 1e-06
clip_limit = 0.1
learn_rate = 0.01
beta_first = 0.9
beta_second = 0.999
adam_eps = 1e-08
weight_decay = 0.05
low_type = jnp.bfloat16
wide = jnp.float32


def product(left, right):
    return jnp.dot(left, right, preferred_element_type=wide)


def product_nt(left, right):
    return jnp.einsum("ab,cb->ac", left, right, preferred_element_type=wide)


def product_tn(left, right):
    return jnp.einsum("ab,ac->bc", left, right, preferred_element_type=wide)


def norm_forward(values, gain, shift):
    center = jnp.mean(values, axis=1, keepdims=True)
    moved = values - center
    inverse = lax.rsqrt(jnp.mean(moved * moved, axis=1, keepdims=True) + norm_eps)
    scaled = moved * inverse
    return scaled * gain + shift, (scaled, inverse)


def norm_backward(upstream, kept, gain):
    scaled, inverse = kept
    inner = upstream * gain
    downstream = inverse * (
        inner
        - jnp.mean(inner, axis=1, keepdims=True)
        - scaled * jnp.mean(inner * scaled, axis=1, keepdims=True)
    )
    return downstream, jnp.sum(upstream * scaled, axis=0), jnp.sum(upstream, axis=0)


def exact_gelu(values):
    return jax.nn.gelu(values, approximate=False)


def split_heads(grouped):
    images = grouped.shape[0] // SEQ
    pieces = grouped.reshape(images, SEQ, 3, HEADS, HD)
    return pieces[:, :, 0], pieces[:, :, 1], pieces[:, :, 2]


def attention_weights(query, keys):
    scores = jnp.einsum("iqhd,ikhd->ihqk", query, keys, preferred_element_type=wide)
    return jax.nn.softmax(scores * (1.0 / math.sqrt(HD)), axis=-1)


def attend(grouped):
    query, keys, values = split_heads(grouped)
    weights_full = attention_weights(query, keys)
    mixture = jnp.einsum(
        "ihqk,ikhd->iqhd", weights_full.astype(low_type), values, preferred_element_type=wide
    )
    return mixture.reshape(grouped.shape[0], HEADS * HD), weights_full


def attend_back(grouped, weights_full, grad_mixture):
    query, keys, values = split_heads(grouped)
    images = query.shape[0]
    weights_low = weights_full.astype(low_type)
    grad_out = grad_mixture.reshape(images, SEQ, HEADS, HD)
    grad_weights = jnp.einsum("iqhd,ikhd->ihqk", grad_out, values, preferred_element_type=wide)
    grad_values = jnp.einsum("ihqk,iqhd->ikhd", weights_low, grad_out, preferred_element_type=wide)
    centered = grad_weights - jnp.sum(weights_full * grad_weights, axis=-1, keepdims=True)
    grad_scores = (weights_full * centered).astype(low_type)
    scale = 1.0 / math.sqrt(HD)
    grad_query = jnp.einsum("ihqk,ikhd->iqhd", grad_scores, keys, preferred_element_type=wide)
    grad_keys = jnp.einsum("ihqk,iqhd->ikhd", grad_scores, query, preferred_element_type=wide)
    stacked = jnp.stack([grad_query * scale, grad_keys * scale, grad_values], axis=2)
    return stacked.reshape(images * SEQ, 3 * HEADS * HD)


def adam_step(weight, grad, drift, power, factor, step_value):
    scaled = grad * factor
    new_drift = beta_first * drift + (1.0 - beta_first) * scaled
    new_power = beta_second * power + (1.0 - beta_second) * scaled * scaled
    drift_hat = new_drift / (1.0 - jnp.power(beta_first, step_value))
    power_hat = new_power / (1.0 - jnp.power(beta_second, step_value))
    update = -learn_rate * (drift_hat / (jnp.sqrt(power_hat) + adam_eps) + weight_decay * weight)
    return (update, new_drift, new_power)


def on_device(
    pixels,
    mask_places,
    mask_count,
    targets,
    step_count,
    patch_weight,
    vector_table,
    input_weight,
    output_weight,
    upward_weight,
    downward_weight,
    head_weight,
    drift_patch,
    drift_table,
    drift_input,
    drift_output,
    drift_upward,
    drift_downward,
    drift_head,
    power_patch,
    power_table,
    power_input,
    power_output,
    power_upward,
    power_downward,
    power_head,
):
    rows, cols = lax.axis_size("row"), lax.axis_size("col")
    row_index = lax.axis_index("row")
    col_index = lax.axis_index("col")
    images = mask_places.shape[0] // rows
    width = vector_table.shape[1] * rows

    blocks = [
        patch_weight.astype(low_type),
        input_weight[0].astype(low_type).T,
        output_weight[0].astype(low_type),
        upward_weight[0].astype(low_type).T,
        downward_weight[0].astype(low_type),
    ]
    heights = [block.shape[0] for block in blocks]
    gathered = lax.all_gather(jnp.concatenate(blocks, axis=0), BOTH, axis=0, tiled=False)
    gathered = gathered.reshape(rows, cols, sum(heights), -1)

    def whole(index):
        start = sum(heights[:index])
        part = gathered[:, :, start : start + heights[index]]
        return jnp.transpose(part, (1, 2, 0, 3)).reshape(cols * heights[index], width)

    patch_low, input_turned, output_low, upward_turned, downward_low = map(whole, range(5))
    table = lax.all_gather(vector_table, "row", axis=1, tiled=True)

    local_images = pixels.shape[0] // SEQ
    part = pixels.shape[1]
    grid = pixels.reshape(local_images // (rows * images), rows, images, SEQ, part)
    grid = lax.all_to_all(grid, "row", split_axis=1, concat_axis=0, tiled=True)
    grid = grid.reshape(cols, images * SEQ, part)
    grid = lax.all_to_all(grid, "col", split_axis=0, concat_axis=0, tiled=True)
    pixel_own = jnp.transpose(grid, (1, 0, 2)).reshape(images * SEQ, cols * part)

    def own(values):
        return lax.dynamic_slice_in_dim(values, row_index * images, images, axis=0)

    places_own, count_own = own(mask_places), own(mask_count)

    def gains_of(norm_index):
        return (table[SEQ + 2 + 2 * norm_index], table[SEQ + 3 + 2 * norm_index])

    patch_proj = product(pixel_own, patch_low)
    places = jnp.arange(SEQ, dtype=jnp.int32)
    counted_own = jnp.arange(MSLOT, dtype=jnp.int32)[None, :] < count_own[:, None]
    matches = places_own[:, :, None] == places[None, None, :]
    masked = jnp.any(matches & counted_own[:, :, None], axis=1)[:, :, None]
    opening = (places == 0)[None, :, None]
    stream = jnp.where(
        opening,
        table[SEQ],
        jnp.where(masked, table[SEQ + 1], patch_proj.reshape(images, SEQ, -1)),
    )
    stream = (stream + table[:SEQ][None]).reshape(images * SEQ, -1)
    gain_one, shift_one = gains_of(0)
    gain_two, shift_two = gains_of(1)
    final_gain, final_shift = gains_of(2)
    normed_one, stats_one = norm_forward(stream, gain_one, shift_one)
    normed_one = normed_one.astype(low_type)
    grouped = product_nt(normed_one, input_turned).astype(low_type)
    mixture, weights_full = attend(grouped)
    mixture = mixture.astype(low_type)
    stream_mid = stream + product(mixture, output_low)
    normed_two, stats_two = norm_forward(stream_mid, gain_two, shift_two)
    normed_two = normed_two.astype(low_type)
    hidden_pre = product_nt(normed_two, upward_turned)
    hidden_act = exact_gelu(hidden_pre).astype(low_type)
    stream_last = stream_mid + product(hidden_act, downward_low)
    final_out, final_stats = norm_forward(stream_last, final_gain, final_shift)
    selector = matches.astype(low_type)
    picked = jnp.einsum(
        "ims,isd->imd", selector, final_out.astype(low_type).reshape(images, SEQ, -1),
        preferred_element_type=wide,
    ).astype(low_type)

    picked_wide = lax.all_gather(picked.reshape(images * MSLOT, -1), "row", axis=0, tiled=True)
    head_low = head_weight.astype(low_type)
    logits = product(picked_wide, head_low)
    vocab_local = head_weight.shape[1]
    target_local = targets.reshape(-1) - row_index * vocab_local
    target_hits = target_local[:, None] == jnp.arange(vocab_local, dtype=jnp.int32)[None, :]
    chosen = jnp.sum(jnp.where(target_hits, logits, 0.0), axis=1)
    local_top = jnp.max(logits, axis=1)
    local_sum = jnp.sum(jnp.exp(logits - local_top[:, None]), axis=1)
    pair = lax.all_gather(jnp.stack([local_top, local_sum]), "row", axis=0, tiled=False)
    top_value = jnp.max(pair[:, 0], axis=0)
    exp_total = jnp.sum(pair[:, 1] * jnp.exp(pair[:, 0] - top_value), axis=0)
    log_total = top_value + jnp.log(exp_total)
    counted = jnp.arange(MSLOT, dtype=jnp.int32)[None, :] < mask_count[:, None]
    slot_weight = counted.reshape(-1).astype(wide)
    leader_row = (row_index == 0).astype(wide)
    loss_part = jnp.sum(log_total * slot_weight) * leader_row - jnp.sum(chosen * slot_weight)
    count_part = jnp.sum(mask_count.astype(wide)) * leader_row
    grad_logits = (
        (jnp.exp(logits - log_total[:, None]) - target_hits.astype(wide)) * slot_weight[:, None]
    ).astype(low_type)
    grad_head_local = product_tn(picked_wide, grad_logits)
    grad_head = lax.psum(grad_head_local.astype(low_type), "col").astype(wide)
    grad_picked = lax.psum_scatter(
        product_nt(grad_logits, head_low).astype(low_type),
        "row",
        scatter_dimension=0,
        tiled=True,
    )
    grad_final = jnp.einsum(
        "ims,imd->isd", selector, grad_picked.reshape(images, MSLOT, -1),
        preferred_element_type=wide,
    )

    grad_stream, grad_final_gain, grad_final_shift = norm_backward(
        grad_final.reshape(images * SEQ, -1), final_stats, final_gain
    )
    grad_two = grad_stream.astype(low_type)
    grad_downward = product_tn(hidden_act, grad_two)
    grad_act = product_nt(grad_two, downward_low)
    _, gelu_pull = jax.vjp(exact_gelu, hidden_pre)
    grad_pre = gelu_pull(grad_act)[0].astype(low_type)
    grad_upward_turned = product_tn(grad_pre, normed_two)
    grad_normed_two = product(grad_pre, upward_turned)
    grad_mid, grad_gain_two, grad_shift_two = norm_backward(grad_normed_two, stats_two, gain_two)
    grad_mid = grad_mid + grad_stream
    grad_one = grad_mid.astype(low_type)
    grad_output = product_tn(mixture, grad_one)
    grad_mixture = product_nt(grad_one, output_low).astype(low_type)
    grad_grouped = attend_back(grouped, weights_full, grad_mixture).astype(low_type)
    grad_input_turned = product_tn(grad_grouped, normed_one)
    grad_normed_one = product(grad_grouped, input_turned)
    grad_below, grad_gain_one, grad_shift_one = norm_backward(grad_normed_one, stats_one, gain_one)
    grad_grid = (grad_below + grad_mid).reshape(images, SEQ, -1)
    grad_patch = jnp.where(opening | masked, 0.0, grad_grid).reshape(images * SEQ, -1)
    grad_patch_weight = product_tn(pixel_own, grad_patch.astype(low_type))
    lines = [
        jnp.sum(grad_grid, axis=0),
        jnp.sum(grad_grid[:, 0], axis=0)[None],
        jnp.sum(jnp.where(masked, grad_grid, 0.0), axis=(0, 1))[None],
        jnp.stack(
            [grad_gain_one, grad_shift_one, grad_gain_two, grad_shift_two,
             grad_final_gain, grad_final_shift]
        ),
    ]
    table_local = jnp.concatenate(lines, axis=0).astype(low_type)

    def dealt(value, height):
        grid = value.astype(low_type).reshape(cols, height, rows, -1)
        return jnp.transpose(grid, (2, 0, 1, 3)).reshape(rows * cols, height, -1)

    stacked = jnp.concatenate(
        [
            dealt(value, height)
            for value, height in zip(
                [grad_patch_weight, grad_input_turned, grad_output, grad_upward_turned,
                 grad_downward],
                heights,
            )
        ],
        axis=1,
    )
    summed = lax.psum_scatter(stacked, BOTH, scatter_dimension=0, tiled=False).astype(wide)
    starts = [sum(heights[:index]) for index in range(6)]
    pieces = [summed[starts[index] : starts[index + 1]] for index in range(5)]
    grad_table = lax.psum(table_local, BOTH).astype(wide)
    grad_table = lax.dynamic_slice_in_dim(
        grad_table, row_index * vector_table.shape[1], vector_table.shape[1], axis=1
    )
    leader_col = (col_index == 0).astype(wide)
    squares_part = jnp.sum(summed * summed) + leader_col * (
        jnp.sum(grad_table * grad_table) + jnp.sum(grad_head * grad_head)
    )
    loss_total, count_total, squares_total = lax.psum((loss_part, count_part, squares_part), BOTH)
    mean_loss = loss_total / count_total
    grad_norm = jnp.sqrt(squares_total) / count_total
    factor = jnp.minimum(1.0, clip_limit / grad_norm) / count_total
    step_value = step_count[0].astype(wide)
    steps = [
        (patch_weight, pieces[0], drift_patch, power_patch),
        (vector_table, grad_table, drift_table, power_table),
        (input_weight, pieces[1].T[None], drift_input, power_input),
        (output_weight, pieces[2][None], drift_output, power_output),
        (upward_weight, pieces[3].T[None], drift_upward, power_upward),
        (downward_weight, pieces[4][None], drift_downward, power_downward),
        (head_weight, grad_head, drift_head, power_head),
    ]
    results = []
    for weight, grad, drift, power in steps:
        results.extend(adam_step(weight, grad, drift, power, factor, step_value))
    return (mean_loss, grad_norm, *results)


def solution(mesh):
    state = (
        P("col", "row"),
        P(None, "row"),
        P(None, "row", "col"),
        P(None, "col", "row"),
        P(None, "row", "col"),
        P(None, "col", "row"),
        P(None, "row"),
    )
    data = (P("row", "col"), P("col", None), P("col"), P("col", None), P())
    outs = (P(), P()) + tuple(spec for spec in state for _ in range(3))
    return jax.shard_map(
        on_device,
        mesh=mesh,
        in_specs=data + state * 3,
        out_specs=outs,
        check_vma=False,
    )
```

time: 1880 us -> 814 us (0.43)
  blocking collectives: 723 us -> 66.4 us
  waiting for transfers between devices: 795 us -> 449 us
  matrix products: 101 us -> 58.1 us
  local copies, waits for them, and re-layouts: 108 us -> 134 us
  starting transfers between devices: 36.3 us -> 10.8 us
    unnamed x6 -> x0, blocking collectives: 526 us -> none
    unnamed x24 -> x5, waiting for transfers between devices: 294 us -> 0.08 us
    all_gather x8 -> x1, waiting for transfers between devices: 378 us -> 86.4 us  [on_device(): lax.all_gather(jnp.concatenate(blocks, axis=0), BOTH, axis=0, tiled=False)]
    reduce_scatter x0 -> x2, waiting for transfers between devices: none -> 176 us  [the longest x1 167 us: on_device(): lax.psum_scatter(stacked, BOTH, scatter_dimension=0, tiled=False)]
    all_to_all x4 -> x0, blocking collectives: 101 us -> none  [image_swap(): lax.all_to_all(values, 'col', split_axis=0, concat_axis=0, tiled=True)]
    psum x1 -> x2, waiting for transfers between devices: 123 us -> 186 us  [the longest x1 143 us: on_device(): grad_head = lax.psum(grad_head_local.astype(low_type), 'col').astype(wide)]
    unnamed x10 -> x0, starting transfers between devices: 35.7 us -> none
    psum x7 -> x1, blocking collectives: 69 us -> 39.5 us  [on_device(): lax.psum((loss_part, count_part, squares_part), BOTH)]
  transfers between devices with their start and end apart: 19 -> 7, of which waited for: 16 -> 5; matrix products, arithmetic and copies ran while one was open for 2% -> 14% of each run, Pallas kernels for 0% -> 0%
where the time goes in v1:
time: 814 us; the launch traced here: 804 us
  waiting for transfers between devices  449 us (55%)
  local copies, waits for them, and re-layouts  134 us (16%)
  blocking collectives  66.4 us (8%)
  other arithmetic  59.5 us (7%)
  matrix products  58.1 us (7%)
  between operations  26.4 us (3%)
  starting transfers between devices  10.8 us (1%)
    reduce_scatter x1, waiting for transfers between devices, on_device(): lax.psum_scatter(stacked, BOTH, scatter_dimension=0, tiled=False)  167 us
    psum x1, waiting for transfers between devices, on_device(): grad_head = lax.psum(grad_head_local.astype(low_type), 'col').astype(wide)  143 us
    all_gather x1, waiting for transfers between devices, on_device(): lax.all_gather(jnp.concatenate(blocks, axis=0), BOTH, axis=0, tiled=False)  86.4 us
    unnamed x198, local copies, waits for them, and re-layouts  51.5 us
    psum x1, waiting for transfers between devices, on_device(): grad_table = lax.psum(table_local, BOTH).astype(wide)  43.2 us
    psum x1, blocking collectives, on_device(): lax.psum((loss_part, count_part, squares_part), BOTH)  39.5 us
    mul x7, other arithmetic, adam_step(): -learn_rate  35 us
    reshape x5, local copies, waits for them, and re-layouts, dealt(): grid = value.astype(low_type).reshape(cols, height, rows, -1)  30.7 us
  transfers between devices with their start and end apart: 7, of which 5 were waited for; matrix products, arithmetic and copies ran while one was open for 14% of the time, Pallas kernels for 0%

profile of v1, /device:TPU:0, one launch (start us, length us, event | category | flops | bytes accessed | tf_op | source)
XLA Modules:
  0.0 804.0 jit_solution(17140014691448463150)
XLA Ops:
  15.8 4.2 all-to-all-start
  21.4 16.2 %all_gather.18 = f32[205,768]{1,0:T(8,128)S(1)} all-gather(f32[205,384]{1,0:T(8,128)S(1)} %copy-done.33), channel_id=1, replica_groups=mesh['row'=2,'col'=16] {'row'}, dimensions={1}, use_global_device_ids=true | all-gather | bytes 944640 | tf_op jit(solution)/shard_map/all_gather | solution.py:157
  38.8 6.1 all-to-all-start.1
  45.0 86.4 %all-gather.5.cloned.1.call-done = bf16[19968,384]{1,0:T(8,128)(2,1)} async-done(((bf16[624,384]{1,0:T(8,128)(2,1)}), bf16[19968,384]{1,0:T(8,128)(2,1)}) %all-gather.5.cloned.1.call-update) | async-done | bytes 15335440 | tf_op jit(solution)/shard_map/all_gather | solution.py:148
  138.1 3.6 copy.146
  144.1 8.6 %fusion.85 = (bf16[2,16,192,384]{3,2,1,0:T(8,128)(2,1)}, bf16[2,16,192,384]{3,2,1,0:T(8,128)(2,1)}) fusion(bf16[2,16,624,384]{3,2,1,0:T(8,128)(2,1)} %bitcast.239), kind=kLoop, calls=%fused_computation.207 | loop fusion | bytes 18874368 | tf_op jit(solution)/shard_map/slice | solution.py:153
  155.3 3.3 convolution_convert_fusion.4
  165.5 9.8 %copy.148 = bf16[2,16,192,384]{3,0,2,1:T(2,128)(2,1)} copy(bf16[2,16,192,384]{3,2,1,0:T(8,128)(2,1)} %get-tuple-element.77) | data formatting | bytes 9437184
  175.3 5.5 copy.154
  183.0 9.8 %copy.149 = bf16[2,16,192,384]{3,0,2,1:T(2,128)(2,1)} copy(bf16[2,16,192,384]{3,2,1,0:T(8,128)(2,1)} %get-tuple-element.76) | data formatting | bytes 9437184
  192.8 3.1 copy.155
  196.0 11.2 %multiply_convert_fusion.2 = (bf16[197,3072]{1,0:T(8,128)(2,1)S(1)}, f32[197,3072]{1,0:T(8,128)}, f32[197,3072]{1,0:T(8,128)}) fusion(bf16[3072,768]{1,0:T(8,128)(2,1)} %bitcast.254, f32[197,768]{1,0:T(8,128)S(1)} %get-tuple-element.88, f32[768]{0:T(1024)S(1)} %get-tuple-element.33, f32[768]{0:T(1024)S(1)} %get-tuple-element.34, ...), kind=kOutput, calls=%fused_computation.27 | convolution fusion | flops 969656064 | bytes 11383336 | tf_op jit(solution)/shard_map/ab,cb->ac/dot_general | solution.py:30
  209.2 6.1 all_gather.21
  217.7 4.5 all-gather.2
  226.1 9.8 %reduce-scatter.3.cloned.1.call-done = bf16[80,768]{1,0:T(8,128)(2,1)} async-done(((bf16[160,768]{1,0:T(8,128)(2,1)}), bf16[80,768]{1,0:T(8,128)(2,1)}) %reduce-scatter.3.cloned.1.call-update) | async-done | bytes 122896 | tf_op jit(solution)/shard_map/reduce_scatter | solution.py:231
  239.8 5.3 add_convert_fusion
  263.1 4.1 concatenate.18
  267.2 5.7 convolution_convert_fusion
  281.9 7.9 reshape.623
  289.8 4.3 copy.136
  298.5 3.8 convolution_convert_fusion.2
  302.3 10.1 %reshape.627 = bf16[16,192,2,384]{3,2,1,0:T(2,128)(2,1)} reshape(bf16[3072,768]{1,0:T(8,128)(2,1)} %convolution_convert_fusion.2) | data formatting | bytes 9437184 | tf_op jit(solution)/shard_map/reshape | solution.py:276
  312.4 5.6 copy.138
  318.0 3.7 convolution_convert_fusion.1
  321.7 10.3 %reshape.629 = bf16[16,192,2,384]{3,2,1,0:T(2,128)(2,1)} reshape(bf16[3072,768]{1,0:T(8,128)(2,1)} %convolution_convert_fusion.1) | data formatting | bytes 9437184 | tf_op jit(solution)/shard_map/reshape | solution.py:276
  332.0 3.5 copy.139
  349.7 43.2 %all-reduce.4.cloned.1.call-done = bf16[205,768]{1,0:T(8,128)(2,1)} async-done(((bf16[205,768]{1,0:T(8,128)(2,1)}), bf16[205,768]{1,0:T(8,128)(2,1)}) %all-reduce.4.cloned.1.call-update) | async-done | bytes 314896 | tf_op jit(solution)/shard_map/psum | solution.py:293
  394.6 142.9 %all-reduce.6.cloned.1.call-done = bf16[768,4096]{1,0:T(8,128)(2,1)} async-done(((bf16[768,4096]{1,0:T(8,128)(2,1)}), bf16[768,4096]{1,0:T(8,128)(2,1)}) %all-reduce.6.cloned.1.call-update) | async-done | bytes 6291472 | tf_op jit(solution)/shard_map/psum | solution.py:230
  537.5 6.6 fusion.3
  545.6 166.7 %reduce-scatter.5.cloned.1.call-done = bf16[1,624,384]{2,1,0:T(8,128)(2,1)} async-done(((bf16[32,624,384]{2,1,0:T(8,128)(2,1)}), bf16[1,624,384]{2,1,0:T(8,128)(2,1)}) %reduce-scatter.5.cloned.1.call-update) | async-done | bytes 479248 | tf_op jit(solution)/shard_map/reduce_scatter | solution.py:290
  714.8 39.5 %all-reduce = (f32[]{:T(128)}, f32[]{:T(128)}, f32[]{:T(128)}) all-reduce(f32[]{:T(128)S(6)} %sub.160, f32[]{:T(128)S(6)} %mul.642, f32[]{:T(128)S(6)} %add.237), channel_id=1, replica_groups=mesh['row'=2,'col'=16] {'row','col'}, use_global_device_ids=true, to_apply=%region_16.17 | all-reduce | flops 3 | bytes 24 | tf_op jit(solution)/shard_map/psum | solution.py:301
  765.2 29.5 %add_multiply_fusion = (f32[768,4096]{1,0:T(8,128)}, f32[768,4096]{1,0:T(8,128)}, f32[768,4096]{1,0:T(8,128)}) fusion(f32[768,4096]{1,0:T(8,128)} %param.37, f32[]{:T(128)} %bitcast.60, f32[]{:T(128)} %bitcast.59, f32[]{:T(128)S(6)} %div.165, bf16[768,4096]{1,0:T(8,128)(2,1)} %all-reduce.6.cloned.1.call-done, f32[768,4096]{1,0:T(8,128)} %param.51, ...), kind=kLoop, calls=%fused_computation.8 | loop fusion | flops 50331648 | bytes 81788944 | tf_op jit(solution)/shard_map/mul | solution.py:102
  (300 shorter events, 96.5 us)
Async XLA Ops:
  7.2 124.2 %all-gather.5.cloned.1.call-start = ((), (), s32[]{:S(2)}) async-start(), calls=%async_computation.8 | async-start | bytes 15814656 | tf_op jit(solution)/shard_map/all_gather | solution.py:148
  8.2 29.5 %copy-start.78 = (s32[2,80]{1,0:T(2,128)S(1)}, s32[2,80]{1,0:T(2,128)}, u32[]{:S(2)}) copy-start(s32[2,80]{1,0:T(2,128)} %param.29) | copy-start | bytes 1924
  15.8 22.2 %all-to-all-start = ((bf16[8,2,1,197,48]{3,0,4,2,1:T(8,128)(2,1)}), bf16[8,2,1,197,48]{3,0,4,2,1:T(8,128)(2,1)S(1)}, u32[]{:S(2)}, u32[]{:S(2)}) async-start(bf16[8,2,1,197,48]{3,0,4,2,1:T(8,128)(2,1)} %copy.121), calls=%async_computation | async-start | bytes 786432 | tf_op jit(solution)/shard_map/all_to_all | solution.py:162
  21.4 132.0 %copy-start.79 = (pred[197]{0:T(512)(128)(4,1)}, pred[197]{0:T(512)(128)(4,1)S(1)}, u32[]{:S(2)}) copy-start(pred[197]{0:T(512)(128)(4,1)S(1)} %fusion.60) | copy-start | bytes 595
  37.6 93.8 %copy-start.38 = (f32[205,768]{1,0:T(8,128)}, f32[205,768]{1,0:T(8,128)S(1)}, u32[]{:S(2)}) copy-start(f32[205,768]{1,0:T(8,128)S(1)} %all_gather.18) | copy-start | bytes 1889284
  37.9 185.0 %copy-start.62 = (s32[160]{0:T(256)}, s32[160]{0:T(256)S(1)}, u32[]{:S(2)}) copy-start(s32[160]{0:T(256)S(1)} %sub.159) | copy-start | bytes 1924
  37.9 185.0 %copy-start.73 = (f32[160]{0:T(256)}, f32[160]{0:T(256)S(1)}, u32[]{:S(2)}) copy-start(f32[160]{0:T(256)S(1)} %convert_element_type.195) | copy-start | bytes 1924
  38.0 158.0 %copy-start.65 = (f32[768]{0:T(1024)}, f32[768]{0:T(1024)S(1)}, u32[]{:S(2)}) copy-start(f32[768]{0:T(1024)S(1)} %get-tuple-element.33) | copy-start | bytes 9220
  38.8 113.9 %all-to-all-start.1 = ((bf16[16,197,48]{1,2,0:T(8,128)(2,1)}), bf16[16,197,48]{1,2,0:T(8,128)(2,1)S(1)}, u32[]{:S(2)}, u32[]{:S(2)}) async-start(bf16[16,197,48]{1,2,0:T(8,128)(2,1)} %bitcast.12), calls=%async_computation.1 | async-start | bytes 786432 | tf_op jit(solution)/shard_map/all_to_all | solution.py:164
  45.0 190.9 %reduce-scatter.3.cloned.1.call-start = ((), (), s32[]{:S(2)}) async-start(), calls=%async_computation.4 | async-start | bytes 368640 | tf_op jit(solution)/shard_map/reduce_scatter | solution.py:231
  182.7 24.4 %copy-start.3 = (f32[197,768]{1,0:T(8,128)}, f32[197,768]{1,0:T(8,128)S(1)}, u32[]{:S(2)}) copy-start(f32[197,768]{1,0:T(8,128)S(1)} %get-tuple-element.88) | copy-start | bytes 1815556
  182.7 64.3 %copy-start.63 = (f32[197]{0:T(256)}, f32[197]{0:T(256)S(1)}, u32[]{:S(2)}) copy-start(f32[197]{0:T(256)S(1)} %broadcast_multiply_fusion.7) | copy-start | bytes 2368
  183.0 64.1 %copy-start.70 = (f32[197]{0:T(256)}, f32[197]{0:T(256)S(1)}, u32[]{:S(2)}) copy-start(f32[197]{0:T(256)S(1)} %add_rsqrt_fusion.1) | copy-start | bytes 2368
  195.9 19.5 %slice-start = ((s8[12582912]{0:T(1024)(128)(4,1)}), s8[4194304]{0:T(1024)(128)(4,1)S(1)}, s32[]{:S(2)}) async-start(s8[12582912]{0:T(1024)(128)(4,1)} %bitcast.225), calls=%async_computation.9 | async-start | bytes 8388608
  195.9 19.5 %slice-start.1 = ((s8[12582912]{0:T(1024)(128)(4,1)}), s8[4194304]{0:T(1024)(128)(4,1)S(1)}, s32[]{:S(2)}) async-start(s8[12582912]{0:T(1024)(128)(4,1)} %bitcast.225), calls=%async_computation.10 | async-start | bytes 8388608
  196.0 19.4 %slice-start.2 = ((s8[12582912]{0:T(1024)(128)(4,1)}), s8[4194304]{0:T(1024)(128)(4,1)S(1)}, s32[]{:S(2)}) async-start(s8[12582912]{0:T(1024)(128)(4,1)} %bitcast.225), calls=%async_computation.11 | async-start | bytes 8388608
  226.1 166.9 %all-reduce.4.cloned.1.call-start = ((), (), s32[]{:S(2)}) async-start(), calls=%async_computation.6 | async-start | bytes 638976 | tf_op jit(solution)/shard_map/psum | solution.py:293
  267.2 270.3 %all-reduce.6.cloned.1.call-start = ((), (), s32[]{:S(2)}) async-start(), calls=%async_computation.7 | async-start | bytes 12582912 | tf_op jit(solution)/shard_map/psum | solution.py:230
  272.9 439.4 %reduce-scatter.5.cloned.1.call-start = ((), (), s32[]{:S(2)}) async-start(), calls=%async_computation.5 | async-start | bytes 15814656 | tf_op jit(solution)/shard_map/reduce_scatter | solution.py:290
  394.5 365.0 %copy-start.45 = (f32[48,384]{1,0:T(8,128)S(1)}, f32[48,384]{1,0:T(8,128)}, u32[]{:S(2)}) copy-start(f32[48,384]{1,0:T(8,128)} %param.31) | copy-start | bytes 221188
  394.5 365.0 %copy-start.53 = (f32[48,384]{1,0:T(8,128)S(1)}, f32[48,384]{1,0:T(8,128)}, u32[]{:S(2)}) copy-start(f32[48,384]{1,0:T(8,128)} %param.45) | copy-start | bytes 221188
  394.6 365.1 %copy-start.54 = (f32[48,384]{1,0:T(8,128)S(1)}, f32[48,384]{1,0:T(8,128)}, u32[]{:S(2)}) copy-start(f32[48,384]{1,0:T(8,128)} %param.38) | copy-start | bytes 221188
  544.1 216.2 %copy-start.37 = (f32[1,384,144]{1,2,0:T(8,128)S(1)}, f32[1,384,144]{1,2,0:T(8,128)}, u32[]{:S(2)}) copy-start(f32[1,384,144]{1,2,0:T(8,128)} %param.33) | copy-start | bytes 663556
  544.1 216.2 %copy-start.51 = (f32[1,384,144]{1,2,0:T(8,128)S(1)}, f32[1,384,144]{1,2,0:T(8,128)}, u32[]{:S(2)}) copy-start(f32[1,384,144]{1,2,0:T(8,128)} %param.47) | copy-start | bytes 663556
  544.1 216.2 %copy-start.52 = (f32[1,384,144]{1,2,0:T(8,128)S(1)}, f32[1,384,144]{1,2,0:T(8,128)}, u32[]{:S(2)}) copy-start(f32[1,384,144]{1,2,0:T(8,128)} %param.40) | copy-start | bytes 663556
  544.1 217.1 %copy-start.46 = (f32[1,48,384]{2,1,0:T(8,128)S(1)}, f32[1,48,384]{2,1,0:T(8,128)}, u32[]{:S(2)}) copy-start(f32[1,48,384]{2,1,0:T(8,128)} %param.34) | copy-start | bytes 221188
  544.1 217.1 %copy-start.55 = (f32[1,48,384]{2,1,0:T(8,128)S(1)}, f32[1,48,384]{2,1,0:T(8,128)}, u32[]{:S(2)}) copy-start(f32[1,48,384]{2,1,0:T(8,128)} %param.48) | copy-start | bytes 221188
  544.1 217.1 %copy-start.56 = (f32[1,48,384]{2,1,0:T(8,128)S(1)}, f32[1,48,384]{2,1,0:T(8,128)}, u32[]{:S(2)}) copy-start(f32[1,48,384]{2,1,0:T(8,128)} %param.41) | copy-start | bytes 221188
  544.1 217.9 %copy-start.35 = (f32[1,384,192]{1,2,0:T(8,128)S(1)}, f32[1,384,192]{1,2,0:T(8,128)}, u32[]{:S(2)}) copy-start(f32[1,384,192]{1,2,0:T(8,128)} %param.35) | copy-start | bytes 884740
  544.1 217.9 %copy-start.47 = (f32[1,384,192]{1,2,0:T(8,128)S(1)}, f32[1,384,192]{1,2,0:T(8,128)}, u32[]{:S(2)}) copy-start(f32[1,384,192]{1,2,0:T(8,128)} %param.49) | copy-start | bytes 884740
  544.2 217.9 %copy-start.48 = (f32[1,384,192]{1,2,0:T(8,128)S(1)}, f32[1,384,192]{1,2,0:T(8,128)}, u32[]{:S(2)}) copy-start(f32[1,384,192]{1,2,0:T(8,128)} %param.42) | copy-start | bytes 884740
  765.2 29.5 %copy-start.1 = (s32[2,80]{1,0:T(2,128)S(1)}, s32[2,80]{1,0:T(2,128)}, u32[]{:S(2)}) copy-start(s32[2,80]{1,0:T(2,128)} %param.27) | copy-start | bytes 1924
  (67 other events, 296.2 us)
Sparse Core Ops, SparseCore 0:
  13.0 118.3 all-gather.4
  226.2 9.6 reduce-scatter.2
  267.3 125.5 all-reduce.3
  397.4 139.9 all-reduce.5
  543.5 168.7 reduce-scatter.4

commit v2 on v1

--- a/solution.py
+++ b/solution.py
@@ -3,6 +3,8 @@
 import jax
 import jax.numpy as jnp
 from jax import lax
+from jax.experimental import pallas as pl
+from jax.experimental.pallas import tpu as pltpu
 from jax.sharding import PartitionSpec as P
 
 HEADS = 12
@@ -318,6 +320,938 @@
     return (mean_loss, grad_norm, *results)
 
 
+VMEM_LIMIT = 62 * 2**20
+TOK = 208
+UNIT = 48
+UNITS = 13
+BANDS = 8
+EYE = pl.DeviceIdType.MESH
+
+
+def nn(left, right):
+    return jnp.dot(left, right, preferred_element_type=wide)
+
+
+def nt(left, right):
+    return lax.dot_general(left, right, (((1,), (1,)), ((), ())), preferred_element_type=wide)
+
+
+def tn(left, right):
+    return lax.dot_general(left, right, (((0,), (0,)), ((), ())), preferred_element_type=wide)
+
+
+def gelu_parts(values):
+    phi_total = 0.5 * (1.0 + lax.erf(values * math.sqrt(0.5)))
+    density = jnp.exp(values * values * -0.5) * (1.0 / math.sqrt(2.0 * math.pi))
+    return phi_total, density
+
+
+def normed(values, gain, shift):
+    center = jnp.mean(values, axis=1, keepdims=True)
+    moved = values - center
+    inverse = lax.rsqrt(jnp.mean(moved * moved, axis=1, keepdims=True) + norm_eps)
+    scaled = moved * inverse
+    return scaled * gain + shift, scaled, inverse
+
+
+def normed_back(upstream, scaled, inverse, gain):
+    inner = upstream * gain
+    down = inverse * (
+        inner
+        - jnp.mean(inner, axis=1, keepdims=True)
+        - scaled * jnp.mean(inner * scaled, axis=1, keepdims=True)
+    )
+    return (
+        down,
+        jnp.sum(upstream * scaled, axis=0, keepdims=True),
+        jnp.sum(upstream, axis=0, keepdims=True),
+    )
+
+
+def step_kernel(
+    pix_in, blk_in, tab_in, places, info_in, counts, head_in,
+    gout, gtab_out, ghead, scal_out,
+    wg, px, tb, st0, st1, st2, n1, n2, mix, qkv, hpre, hact,
+    hn, hbuf, pk, pkp, pp, lt, pkt, gch, colb, sq, lsb, flip, tmpa, gpk, gps, gpr, g2b, gacc, gst,
+    rk, r1a, r1b, r2a, r2b, rz, tab, tabk, tabr, fin,
+    ag_send, ag_recv, px_send, px_recv, tb_sem, pk_send, pk_recv, ex_send, ex_recv,
+    ls_send, ls_recv, rs_send, rs_recv, tab_send, tab_recv, fin_send, fin_recv, hb_sem, gh_sem,
+):
+    r = lax.axis_index("row")
+    c = lax.axis_index("col")
+    z, x, k = c // 4, (c // 2) % 2, c % 2
+    half = tb.shape[1] // 2
+    d_y = (1 - r, c)
+    d_x = (r, z * 4 + (1 - x) * 2 + k)
+    d_k = (r, z * 4 + x * 2 + 1 - k)
+
+    def d_z(step):
+        return (r, lax.rem(z + step, 4) * 4 + x * 2 + k)
+
+    def remote(src, dst, send, recv, device):
+        return pltpu.make_async_remote_copy(
+            src_ref=src, dst_ref=dst, send_sem=send, recv_sem=recv,
+            device_id=device, device_id_type=EYE,
+        )
+
+    def lanes(row):
+        return pl.ds(pl.multiple_of(row * half, half), half)
+
+    sq[...] = jnp.zeros_like(sq)
+    barrier = pltpu.get_barrier_semaphore()
+
+    def greet(n, _):
+        other = lax.rem(r * 16 + c + n, 32)
+        pl.semaphore_signal(barrier, inc=1, device_id=(other // 16, other % 16), device_id_type=EYE)
+        return 0
+
+    lax.fori_loop(1, 32, greet, 0)
+
+    for n in range(UNITS):
+        wg[z, x, k, UNIT * n : UNIT * (n + 1), lanes(r)] = blk_in[UNIT * n : UNIT * (n + 1)]
+    tb[:, lanes(r)] = tab_in[...]
+    hcopy = lambda n: pltpu.make_async_copy(
+        head_in.at[:, pl.ds(pl.multiple_of(n * 256, 256), 256)], hbuf.at[n % 2], hb_sem.at[n % 2]
+    )
+    hcopy(0).start()
+    pl.semaphore_wait(barrier, 31)
+
+    def gather_moves(buf, part, both, send, recv):
+        lo, hi = pl.ds(0, 2), pl.ds(2, 2)
+        every = slice(None)
+        other = lax.rem
+
+        def move(index, out_region, in_region, device):
+            out_ref = buf.at[out_region]
+            in_ref = buf.at[in_region]
+            return (
+                remote(out_ref, out_ref, send.at[index], recv.at[index], device),
+                remote(in_ref, in_ref, send.at[index], recv.at[index], device),
+            )
+
+        first = [
+            move(n - 1, (z, x, k) + part(r), (lax.rem(z + 4 - n, 4), x, k) + part(r), d_z(n))
+            for n in (1, 2, 3)
+        ]
+        second = [
+            move(3, (lo, x, k) + part(r), (lo, 1 - x, k) + part(r), d_x),
+            move(4, (hi, x, k) + part(r), (hi, x, k) + part(1 - r), d_y),
+        ]
+        pair_one = [move(5, (every, x, k) + part(r), (every, x, 1 - k) + part(r), d_k)]
+        third = [
+            move(6, (lo, every, k) + part(r), (lo, every, k) + part(1 - r), d_y),
+            move(7, (hi, x, k) + both, (hi, 1 - x, k) + both, d_x),
+        ]
+        pair_two = [
+            move(8, (lo, 1 - x, k) + part(r), (lo, 1 - x, 1 - k) + part(r), d_k),
+            move(9, (hi, x, k) + part(1 - r), (hi, x, 1 - k) + part(1 - r), d_k),
+        ]
+        pair_three = [
+            move(10, (lo, every, k) + part(1 - r), (lo, every, 1 - k) + part(1 - r), d_k),
+            move(11, (hi, 1 - x, k) + both, (hi, 1 - x, 1 - k) + both, d_k),
+        ]
+        return first, second, pair_one, third, pair_two, pair_three
+
+    def begin(moves):
+        for out_copy, _ in moves:
+            out_copy.start()
+
+    def landed(moves):
+        for _, in_copy in moves:
+            in_copy.wait_recv()
+
+    def sent(moves):
+        for out_copy, _ in moves:
+            out_copy.wait_send()
+
+    def unit_rows(n):
+        return pl.ds(pl.multiple_of(n * UNIT, UNIT), UNIT)
+
+    def weight_moves(n):
+        rows = unit_rows(n)
+        return gather_moves(
+            wg, lambda row: (rows, lanes(row)), (rows, slice(None)), ag_send.at[n], ag_recv.at[n]
+        )
+
+    def picked_moves(n):
+        cut = lanes(n)
+        return gather_moves(
+            pk, lambda row: (pl.ds(pl.multiple_of(row * MSLOT, 16), MSLOT), cut),
+            (slice(None), cut), pk_send.at[n], pk_recv.at[n],
+        )
+
+    def px_move(n):
+        target = (n % 2, 8 * r + n // 2)
+        slot = pl.ds(pl.multiple_of(c * UNIT, UNIT), UNIT)
+        return target, remote(pix_in.at[n], px.at[slot], px_send.at[n], px_recv.at[c], target)
+
+    def px_in(n):
+        slot = pl.ds(pl.multiple_of(n * UNIT, UNIT), UNIT)
+        return remote(px.at[slot], px.at[slot], px_send.at[n], px_recv.at[n], d_y)
+
+    def px_start(n, _):
+        target, copy = px_move(n)
+        mine = jnp.logical_and(target[0] == r, target[1] == c)
+
+        @pl.when(mine)
+        def _():
+            px[pl.ds(pl.multiple_of(c * UNIT, UNIT), UNIT), :] = pix_in[n]
+
+        @pl.when(jnp.logical_not(mine))
+        def _():
+            copy.start()
+
+        return 0
+
+    def px_done(n, _):
+        target, copy = px_move(n)
+
+        @pl.when(jnp.logical_not(jnp.logical_and(target[0] == r, target[1] == c)))
+        def _():
+            copy.wait_send()
+
+        @pl.when(jnp.logical_not(jnp.logical_and(n == c, r == c // 8)))
+        def _():
+            px_in(n).wait_recv()
+
+        return 0
+
+    cut_rows = TOK // 2
+    own_cut = pl.ds(pl.multiple_of(k * cut_rows, 8), cut_rows)
+    other_cut = pl.ds(pl.multiple_of((1 - k) * cut_rows, 8), cut_rows)
+
+    def tb_copy(rows, row, index, device):
+        ref = tb.at[rows, lanes(row)]
+        return remote(ref, ref, tb_sem.at[index, 0], tb_sem.at[index, 1], device)
+
+    token = lax.broadcasted_iota(jnp.int32, (TOK, 1), 0)
+    slot_hit = lax.broadcasted_iota(jnp.int32, (TOK, MSLOT), 0) == places[pl.ds(r, 1), :]
+    slot_on = lax.broadcasted_iota(jnp.int32, (TOK, MSLOT), 1) < counts[r]
+    selector = jnp.where(slot_hit, 1.0, 0.0)
+    masked = jnp.sum(jnp.where(slot_on, selector, 0.0), axis=1, keepdims=True) > 0.5
+    opening = token == 0
+
+    def gain(n):
+        return tb[SEQ + 2 + 2 * n : SEQ + 3 + 2 * n, :]
+
+    def shift(n):
+        return tb[SEQ + 3 + 2 * n : SEQ + 4 + 2 * n, :]
+
+    def square(n):
+        return wg[:, :, :, unit_rows(n), :].reshape(16 * UNIT, 2 * half)
+
+    def set_square(n, value):
+        wg[:, :, :, unit_rows(n), :] = value.astype(low_type).reshape(4, 2, 2, UNIT, 2 * half)
+
+    def triple():
+        return wg[:, :, :, UNIT : 4 * UNIT, :].reshape(48 * UNIT, 2 * half)
+
+    lane_low = lax.broadcasted_iota(jnp.int32, (1, 2 * HD), 1) < HD
+    keep_low = jnp.where(lane_low, 1.0, 0.0)
+    keep_high = 1.0 - keep_low
+
+    def twice(values):
+        return jnp.concatenate(
+            [values * keep_low.astype(low_type), values * keep_high.astype(low_type)], axis=0
+        )
+
+    def once(values):
+        return values[:TOK] * keep_low + values[TOK:] * keep_high
+
+    def pair_lanes(part, p):
+        return pl.ds(pl.multiple_of(part * HEADS * HD + p * 2 * HD, 2 * HD), 2 * HD)
+
+    def pair_probs(p):
+        query2 = twice(qkv[:, pair_lanes(0, p)])
+        key2 = qkv[:, pair_lanes(1, p)]
+        scores = nt(query2, key2) * (1.0 / math.sqrt(HD))
+        valid = lax.broadcasted_iota(jnp.int32, (1, TOK), 1) < SEQ
+        scores = jnp.where(valid, scores, -1e30)
+        lifted = jnp.exp(scores - jnp.max(scores, axis=1, keepdims=True))
+        return query2, key2, lifted * (1.0 / jnp.sum(lifted, axis=1, keepdims=True))
+
+    def do_patch():
+        tb_copy(own_cut, 1 - r, 0, d_y).wait_recv()
+        tb_copy(own_cut, 1 - r, 1, d_k).start()
+        lax.fori_loop(0, 16, px_done, 0)
+        patch = tn(px[...], square(0))[:TOK]
+        tb_copy(own_cut, r, 0, d_y).wait_send()
+        tb_copy(other_cut, 1 - r, 1, d_k).wait_recv()
+        tb_copy(own_cut, 1 - r, 1, d_k).wait_send()
+        value = jnp.where(
+            opening, tb[SEQ : SEQ + 1, :], jnp.where(masked, tb[SEQ + 1 : SEQ + 2, :], patch)
+        )
+        value = jnp.where(token < SEQ, value + tb[...], 0.0)
+        st0[...] = value
+        n1[...] = normed(value, gain(0), shift(0))[0].astype(low_type)
+
+    def do_attention():
+        qkv[...] = nt(n1[...], triple()).astype(low_type)
+
+        def one_pair(p, _):
+            _, _, probs = pair_probs(p)
+            mixed = nn(probs.astype(low_type), qkv[:, pair_lanes(2, p)])
+            mix[:, pair_lanes(0, p)] = once(mixed).astype(low_type)
+            return 0
+
+        lax.fori_loop(0, HEADS // 2, one_pair, 0)
+
+    def do_output():
+        value = st0[...] + nn(mix[...], square(4))
+        st1[...] = value
+        st2[...] = value
+        n2[...] = normed(value, gain(1), shift(1))[0].astype(low_type)
+
+    def do_up(j):
+        value = nt(n2[...], square(5 + j))
+        hpre[j] = value
+        phi_total, _ = gelu_parts(value)
+        hact[j] = (value * phi_total).astype(low_type)
+
+    def do_down(j):
+        st2[...] += nn(hact[j], square(9 + j))
+
+    begin(weight_moves(0)[0])
+    lax.fori_loop(0, 16, px_start, 0)
+    tb_copy(own_cut, r, 0, d_y).start()
+
+    def tick(t, _):
+        @pl.when(jnp.logical_and(t >= 1, t < UNITS))
+        def _():
+            begin(weight_moves(t)[0])
+
+        @pl.when(jnp.logical_and(t >= 2, t < UNITS + 2))
+        def _():
+            first, second, pair_one, _, _, _ = weight_moves(t - 2)
+            landed(first)
+            begin(second)
+            begin(pair_one)
+
+        @pl.when(jnp.logical_and(t >= 3, t < UNITS + 3))
+        def _():
+            _, second, _, third, pair_two, _ = weight_moves(t - 3)
+            landed(second)
+            begin(third)
+            begin(pair_two)
+
+        @pl.when(jnp.logical_and(t >= 5, t < UNITS + 5))
+        def _():
+            _, _, _, third, _, pair_three = weight_moves(t - 5)
+            landed(third)
+            begin(pair_three)
+
+        @pl.when(t >= 6)
+        def _():
+            _, _, pair_one, _, pair_two, pair_three = weight_moves(t - 6)
+            landed(pair_one)
+            landed(pair_two)
+            landed(pair_three)
+
+        @pl.when(t < 2 * BANDS)
+        def _():
+            @pl.when(t + 1 < 2 * BANDS)
+            def _():
+                hcopy(t + 1).start()
+
+            hcopy(t).wait()
+            hn[:, pl.ds(pl.multiple_of(t * 256, 256), 256)] = hbuf[t % 2].astype(low_type)
+
+        @pl.when(t == 6)
+        def _():
+            do_patch()
+
+        @pl.when(t == 9)
+        def _():
+            do_attention()
+
+        @pl.when(t == 10)
+        def _():
+            do_output()
+
+        @pl.when(jnp.logical_and(t >= 11, t < 15))
+        def _():
+            do_up(t - 11)
+
+        @pl.when(t >= 15)
+        def _():
+            do_down(t - 15)
+
+        return 0
+
+    lax.fori_loop(0, UNITS + 6, tick, 0)
+
+    def all_sent(n, _):
+        for moves in weight_moves(n):
+            sent(moves)
+        return 0
+
+    final_out, _, _ = normed(st2[...], gain(2), shift(2))
+    picked = tn(selector.astype(low_type), final_out.astype(low_type)).astype(low_type)
+    own_rows = pl.ds(pl.multiple_of(r * MSLOT, 16), MSLOT)
+    other_rows = pl.ds(pl.multiple_of((1 - r) * MSLOT, 16), MSLOT)
+    pp[own_rows, :] = picked
+    pk[z, x, k, own_rows, :] = picked
+
+    def swap(index, src, dst, device):
+        return remote(src, dst, ex_send.at[index], ex_recv.at[index], device)
+
+    swap_picked = swap(0, pp.at[own_rows, :], pkp, d_y)
+    swap_picked.start()
+    for n in range(2):
+        begin(picked_moves(n)[0])
+    lax.fori_loop(0, UNITS, all_sent, 0)
+    info = jnp.transpose(info_in[...])
+    target_col = info[: 2 * MSLOT, 1:2]
+    weight_col = info[: 2 * MSLOT, 2:3]
+    base = (r * (BANDS * 512)).astype(wide)
+    band_lane = lax.broadcasted_iota(jnp.int32, (1, 512), 1).astype(wide)
+
+    def band(v):
+        return pl.ds(pl.multiple_of(v * 512, 512), 512)
+
+    def band_hit(v, column):
+        return (band_lane + (base + (v * 512).astype(wide))) == column
+
+    swap_picked.wait()
+    pp[other_rows, :] = pkp[...]
+
+    def picked_second(n):
+        first, second, pair_one, _, _, _ = picked_moves(n)
+        landed(first)
+        begin(second)
+        begin(pair_one)
+
+    def picked_third(n):
+        _, second, _, third, pair_two, _ = picked_moves(n)
+        landed(second)
+        begin(third)
+        begin(pair_two)
+
+    def picked_last(n):
+        _, _, _, third, _, pair_three = picked_moves(n)
+        landed(third)
+        begin(pair_three)
+
+    def picked_done(n):
+        _, _, pair_one, _, pair_two, pair_three = picked_moves(n)
+        landed(pair_one)
+        landed(pair_two)
+        landed(pair_three)
+
+    def logits_band(v, carry):
+        top, chosen = carry
+        value = nn(pp[...], hn[:, band(v)])
+        lt[v] = value
+        chosen += jnp.sum(jnp.where(band_hit(v, target_col), value, 0.0), axis=1, keepdims=True)
+        return jnp.maximum(top, jnp.max(value, axis=1, keepdims=True)), chosen
+
+    zero_col = jnp.zeros((2 * MSLOT, 1), wide)
+    top, chosen = lax.fori_loop(0, BANDS, logits_band, (zero_col - 1e30, zero_col))
+    picked_second(0)
+
+    def sum_band(v, total):
+        return total + jnp.sum(jnp.exp(lt[v] - top), axis=1, keepdims=True)
+
+    total = lax.fori_loop(0, BANDS, sum_band, zero_col)
+    column = lax.broadcasted_iota(jnp.int32, (1, 128), 1)
+    tmpa[...] = jnp.zeros_like(tmpa)
+    tmpa[0 : 2 * MSLOT, :] = jnp.where(column == 0, top, jnp.where(column == 1, total, 0.0))
+    sq[0] = jnp.transpose(tmpa[...])[:8]
+    swap_lse = swap(1, sq.at[0], sq.at[1], d_y)
+    swap_lse.start()
+    picked_second(1)
+    picked_third(0)
+    swap_lse.wait()
+    flip[...] = jnp.zeros_like(flip)
+    flip[0:8, :] = sq[1]
+    theirs = jnp.transpose(flip[...])[: 2 * MSLOT]
+    their_top, their_total = theirs[:, 0:1], theirs[:, 1:2]
+    best = jnp.maximum(top, their_top)
+    log_total = best + jnp.log(total * jnp.exp(top - best) + their_total * jnp.exp(their_top - best))
+
+    tmpa[0 : 2 * MSLOT, :] = jnp.where(
+        column == 0, log_total, jnp.where(column == 1, target_col, jnp.where(column == 2, weight_col, 0.0))
+    )
+    lsb[c] = jnp.transpose(tmpa[...])[:8]
+
+    def ls_copy(n):
+        other = lax.rem(c + n, 16)
+        return remote(lsb.at[c], lsb.at[c], ls_send.at[n], ls_recv.at[n], (r, other))
+
+    def ls_in(n):
+        other = lax.rem(c + 16 - n, 16)
+        return remote(lsb.at[other], lsb.at[other], ls_send.at[n], ls_recv.at[n], (r, other))
+
+    def ls_start(n, _):
+        ls_copy(n).start()
+        return 0
+
+    def ls_done(n, _):
+        ls_copy(n).wait_send()
+        ls_in(n).wait_recv()
+        return 0
+
+    lax.fori_loop(1, 16, ls_start, 0)
+    gpk[...] = jnp.zeros_like(gpk)
+
+    def grad_band(v, _):
+        value = jnp.exp(lt[v] - log_total) - jnp.where(band_hit(v, target_col), 1.0, 0.0)
+        gpk[...] += nt((value * weight_col).astype(low_type), hn[:, band(v)])
+        return 0
+
+    lax.fori_loop(0, BANDS, grad_band, 0)
+    gps[...] = gpk[other_rows, :].astype(low_type)
+    swap_grad = swap(2, gps, gpr, d_y)
+    swap_grad.start()
+    picked_third(1)
+    picked_last(0)
+    leader = jnp.where(r == 0, 1.0, 0.0)
+    loss_part = jnp.sum((log_total * leader - chosen) * weight_col, axis=0, keepdims=True)
+    swap_grad.wait()
+    grad_picked = (gpk[own_rows, :] + gpr[...].astype(wide)).astype(low_type)
+    grad_final = nn(selector.astype(low_type), grad_picked)
+    _, scaled, inverse = normed(st2[...], gain(2), shift(2))
+    grad_last, grad_gain, grad_shift = normed_back(grad_final, scaled, inverse, gain(2))
+    st2[...] = grad_last
+    g2b[...] = grad_last.astype(low_type)
+    gst[4:5, :] = grad_gain
+    gst[5:6, :] = grad_shift
+    gacc[...] = jnp.zeros_like(gacc)
+    picked_last(1)
+
+    def pair_region(n):
+        return rk.at[lax.rem(n, 4)]
+
+    def rs_copy(n, index, src, dst, device):
+        return remote(src, dst, rs_send.at[n, index], rs_recv.at[n, index], device)
+
+    lo, hi = pl.ds(0, 2), pl.ds(2, 2)
+
+    def sums_moves(n):
+        rows = unit_rows(UNITS - 1 - n)
+        zero = [rs_copy(n, 0, wg.at[:, :, 1 - k, rows, :], rk.at[lax.rem(n, 4)], d_k)]
+        one = [
+            rs_copy(n, 1, wg.at[lo, :, k, rows, lanes(1 - r)], r1a.at[lax.rem(n, 7)], d_y),
+            rs_copy(n, 2, wg.at[hi, 1 - x, k, rows, :], r1b.at[lax.rem(n, 7)], d_x),
+        ]
+        two = [
+            rs_copy(n, 3, wg.at[lo, 1 - x, k, rows, lanes(r)], r2a.at[lax.rem(n, 7)], d_x),
+            rs_copy(n, 4, wg.at[hi, x, k, rows, lanes(1 - r)], r2b.at[lax.rem(n, 7)], d_y),
+        ]
+        three = [
+            rs_copy(n, 4 + m, wg.at[lax.rem(z + m, 4), x, k, rows, lanes(r)], rz.at[lax.rem(n, 7), m - 1], d_z(m))
+            for m in (1, 2, 3)
+        ]
+        return zero, one, two, three
+
+    def sum_start(copies):
+        for copy in copies:
+            copy.start()
+
+    def sum_land(copies):
+        for copy in copies:
+            copy.wait_recv()
+
+    def fold(region, value):
+        wg[region] = (wg[region].astype(wide) + value.astype(wide)).astype(low_type)
+
+    def sums_one(n):
+        rows = unit_rows(UNITS - 1 - n)
+        zero, one, _, _ = sums_moves(n)
+        sum_land(zero)
+        fold((slice(None), slice(None), k, rows, slice(None)), rk[lax.rem(n, 4)])
+        sum_start(one)
+
+    def sums_two(n):
+        rows = unit_rows(UNITS - 1 - n)
+        _, one, two, _ = sums_moves(n)
+        sum_land(one)
+        fold((lo, slice(None), k, rows, lanes(r)), r1a[lax.rem(n, 7)])
+        fold((hi, x, k, rows, slice(None)), r1b[lax.rem(n, 7)])
+        sum_start(two)
+
+    def sums_three(n):
+        rows = unit_rows(UNITS - 1 - n)
+        _, _, two, three = sums_moves(n)
+        sum_land(two)
+        fold((lo, x, k, rows, lanes(r)), r2a[lax.rem(n, 7)])
+        fold((hi, x, k, rows, lanes(r)), r2b[lax.rem(n, 7)])
+        sum_start(three)
+
+    def sums_four(n):
+        rows = unit_rows(UNITS - 1 - n)
+        _, _, _, three = sums_moves(n)
+        sum_land(three)
+        value = wg[z, x, k, rows, lanes(r)].astype(wide)
+        for m in range(3):
+            value = value + rz[lax.rem(n, 7), m].astype(wide)
+        gout[rows, :] = value
+        sq[2, 0:1, 0:128] += jnp.sum(jnp.sum(value * value, axis=0, keepdims=True), axis=1, keepdims=True)
+
+    def sums_sent(n, _):
+        for moves in sums_moves(n):
+            sent([(copy, None) for copy in moves])
+        return 0
+
+    def back_down(j):
+        grad_act = nt(g2b[...], square(9 + j))
+        value = hpre[j]
+        phi_total, density = gelu_parts(value)
+        grad_pre = (grad_act * (phi_total + value * density)).astype(low_type)
+        set_square(9 + j, tn(hact[j], g2b[...]))
+        hact[j] = grad_pre
+
+    def back_up(j):
+        gacc[...] += nn(hact[j], square(5 + j))
+        set_square(5 + j, tn(hact[j], n2[...]))
+
+    def back_output():
+        _, scaled, inverse = normed(st1[...], gain(1), shift(1))
+        down, grad_gain, grad_shift = normed_back(gacc[...], scaled, inverse, gain(1))
+        gst[2:3, :] = grad_gain
+        gst[3:4, :] = grad_shift
+        down = down + st2[...]
+        st2[...] = down
+        g2b[...] = down.astype(low_type)
+        grad_mix = nt(g2b[...], square(4)).astype(low_type)
+        set_square(4, tn(mix[...], g2b[...]))
+        mix[...] = grad_mix
+
+    def back_attention():
+        def one_pair(p, _):
+            query2, key2, probs = pair_probs(p)
+            value2 = qkv[:, pair_lanes(2, p)]
+            upstream = twice(mix[:, pair_lanes(0, p)])
+            grad_probs = nt(upstream, value2)
+            centered = grad_probs - jnp.sum(probs * grad_probs, axis=1, keepdims=True)
+            grad_scores = (probs * centered).astype(low_type)
+            scale = 1.0 / math.sqrt(HD)
+            grad_query = once(nn(grad_scores, key2)) * scale
+            grad_key = tn(grad_scores, query2) * scale
+            grad_value = tn(probs.astype(low_type), upstream)
+            qkv[:, pair_lanes(0, p)] = grad_query.astype(low_type)
+            qkv[:, pair_lanes(1, p)] = grad_key.astype(low_type)
+            qkv[:, pair_lanes(2, p)] = grad_value.astype(low_type)
+            return 0
+
+        lax.fori_loop(0, HEADS // 2, one_pair, 0)
+        gacc[...] = nn(qkv[...], triple())
+        wg[:, :, :, UNIT : 4 * UNIT, :] = (
+            tn(qkv[...], n1[...]).astype(low_type).reshape(4, 2, 2, 3 * UNIT, 2 * half)
+        )
+
+    def back_patch():
+        _, scaled, inverse = normed(st0[...], gain(0), shift(0))
+        down, grad_gain, grad_shift = normed_back(gacc[...], scaled, inverse, gain(0))
+        grad = down + st2[...]
+        grad_patch = jnp.where(jnp.logical_or(opening, masked), 0.0, grad).astype(low_type)
+        set_square(0, nn(px[:, 0:TOK], grad_patch))
+        lines = [
+            grad[0:1],
+            jnp.sum(jnp.where(masked, grad, 0.0), axis=0, keepdims=True),
+            grad_gain, grad_shift, gst[2:3, :], gst[3:4, :], gst[4:5, :], gst[5:6, :],
+        ]
+        for n, line in enumerate(lines):
+            grad = jnp.where(token == SEQ + n, line, grad)
+        tab[0:TOK, :] = grad.astype(low_type)
+        tab[TOK:, :] = jnp.zeros((tab.shape[0] - TOK, tab.shape[1]), low_type)
+
+    tab_half = tab.shape[0] // 2
+    rows_own = pl.ds(pl.multiple_of(k * tab_half, 16), tab_half)
+    rows_other = pl.ds(pl.multiple_of((1 - k) * tab_half, 16), tab_half)
+    d_z1 = (r, (z + 1 - 2 * (z % 2)) * 4 + x * 2 + k)
+    d_z2 = (r, lax.rem(z + 2, 4) * 4 + x * 2 + k)
+    own_part = tab.at[rows_own, lanes(r)]
+    tab_moves = [
+        remote(tab.at[rows_other, :], tabk, tab_send.at[0], tab_recv.at[0], d_k),
+        remote(tab.at[rows_own, lanes(1 - r)], tabr.at[0], tab_send.at[1], tab_recv.at[1], d_y),
+        remote(own_part, tabr.at[1], tab_send.at[2], tab_recv.at[2], d_x),
+        remote(own_part, tabr.at[2], tab_send.at[3], tab_recv.at[3], d_z1),
+        remote(own_part, tabr.at[3], tab_send.at[4], tab_recv.at[4], d_z2),
+        remote(own_part, tabr.at[4], tab_send.at[5], tab_recv.at[5], d_k),
+    ]
+
+    def tab_step(n):
+        tab_moves[n].wait()
+        if n == 0:
+            tab[rows_own, :] = (
+                tab[rows_own, :].astype(wide) + tabk[...].astype(wide)
+            ).astype(low_type)
+        elif n < 5:
+            tab[rows_own, lanes(r)] = (
+                tab[rows_own, lanes(r)].astype(wide) + tabr[n - 1].astype(wide)
+            ).astype(low_type)
+        if n < 5:
+            tab_moves[n + 1].start()
+
+    def gh_copy(v):
+        return pltpu.make_async_copy(hn.at[:, band(v)], ghead.at[:, band(v)], gh_sem.at[v])
+
+    def head_band(v):
+        def rows_block(n, _):
+            at = pl.ds(pl.multiple_of(n * 4 * MSLOT, 16), 4 * MSLOT)
+            value = nn(pk[n // 2, n % 2].reshape(4 * MSLOT, 2 * half), hn[:, band(v)])
+            cols = colb[at, :]
+            hit = jnp.where(band_hit(v, cols[:, 1:2]), 1.0, 0.0)
+            gch[at, :] = ((jnp.exp(value - cols[:, 0:1]) - hit) * cols[:, 2:3]).astype(low_type)
+            return 0
+
+        lax.fori_loop(0, 8, rows_block, 0)
+        value = nn(pkt[...], gch[...])
+        sq[3, 0:1, 0:128] += jnp.sum(jnp.sum(value * value, axis=0, keepdims=True), axis=1, keepdims=True)
+        hn[:, band(v)] = value.astype(low_type)
+        gh_copy(v).start()
+
+    def head_ready():
+        for n in range(2):
+            picked_done(n)
+        lax.fori_loop(1, 16, ls_done, 0)
+
+        def to_columns(n, _):
+            flip[0:8, :] = lsb[n]
+            colb[pl.ds(pl.multiple_of(n * 2 * MSLOT, 16), 2 * MSLOT), :] = jnp.transpose(flip[...])[: 2 * MSLOT]
+            return 0
+
+        lax.fori_loop(0, 16, to_columns, 0)
+
+        def turn(n, _):
+            rows = pk[n].reshape(8 * MSLOT, 2 * half)
+            pkt[:, pl.ds(pl.multiple_of(n * 8 * MSLOT, 128), 8 * MSLOT)] = jnp.transpose(rows)
+            return 0
+
+        lax.fori_loop(0, 4, turn, 0)
+
+    def back_step(s, _):
+        @pl.when(s < 4)
+        def _():
+            back_down(3 - s)
+
+        @pl.when(jnp.logical_and(s >= 4, s < 8))
+        def _():
+            back_up(7 - s)
+
+        @pl.when(s == 8)
+        def _():
+            back_output()
+
+        @pl.when(s == 9)
+        def _():
+            back_attention()
+
+        @pl.when(s == 12)
+        def _():
+            back_patch()
+            tab_moves[0].start()
+
+        @pl.when(s < UNITS)
+        def _():
+            sum_start(sums_moves(s)[0])
+
+        @pl.when(jnp.logical_and(s >= 1, s < UNITS + 1))
+        def _():
+            sums_one(s - 1)
+
+        @pl.when(jnp.logical_and(s >= 3, s < UNITS + 3))
+        def _():
+            sums_two(s - 3)
+
+        @pl.when(jnp.logical_and(s >= 5, s < UNITS + 5))
+        def _():
+            sums_three(s - 5)
+
+        @pl.when(s >= 7)
+        def _():
+            sums_four(s - 7)
+
+        for n in range(6):
+            @pl.when(s == 13 + n)
+            def _():
+                tab_step(n)
+
+        @pl.when(s == 2)
+        def _():
+            head_ready()
+
+        @pl.when(jnp.logical_and(s >= 3, s < 7))
+        def _():
+            head_band(s - 3)
+
+        @pl.when(jnp.logical_and(s >= 10, s < 12))
+        def _():
+            head_band(s - 6)
+
+        @pl.when(jnp.logical_and(s >= 13, s < 15))
+        def _():
+            head_band(s - 7)
+
+        return 0
+
+    lax.fori_loop(0, UNITS + 7, back_step, 0)
+    gtab_out[rows_own, :] = tab[rows_own, lanes(r)].astype(wide)
+    gtab_out[rows_other, :] = tabr[4].astype(wide)
+    value = gtab_out[...]
+    first_col = jnp.where(c == 0, 1.0, 0.0)
+    table_squares = jnp.sum(jnp.sum(value * value, axis=0, keepdims=True), axis=1, keepdims=True)
+    line = lax.broadcasted_iota(jnp.int32, (8, 128), 0)
+    squares = sq[2, 0:1, 0:128] + (sq[3, 0:1, 0:128] + table_squares) * first_col
+    count = (counts[0] + counts[1]).astype(wide) * leader
+    fin[r * 16 + c] = jnp.where(
+        line == 0, loss_part, jnp.where(line == 1, count, jnp.where(line == 2, squares, 0.0))
+    )
+
+    def fin_copy(n, step):
+        other = lax.rem(r * 16 + c + step, 32)
+        owner = r * 16 + c if n == 0 else lax.rem(r * 16 + c + 32 - step, 32)
+        ref = fin.at[owner]
+        return remote(ref, ref, fin_send.at[step], fin_recv.at[step], (other // 16, other % 16))
+
+    def fin_start(step, _):
+        fin_copy(0, step).start()
+        return 0
+
+    def fin_done(step, _):
+        fin_copy(0, step).wait_send()
+        fin_copy(1, step).wait_recv()
+        return 0
+
+    lax.fori_loop(1, 32, fin_start, 0)
+    lax.fori_loop(0, UNITS, sums_sent, 0)
+    for n in range(2):
+        for moves in picked_moves(n):
+            sent(moves)
+    for v in range(BANDS):
+        gh_copy(v).wait()
+    lax.fori_loop(1, 32, fin_done, 0)
+    scal_out[...] = jnp.sum(fin[...], axis=0)
+
+
+def step_call(pix, blk, tab, places, info, counts, head):
+    half = tab.shape[1]
+    full = 2 * half
+    vocab = head.shape[1]
+    slots = 32 * MSLOT
+    vm = pltpu.VMEM
+    dma = pltpu.SemaphoreType.DMA
+    f32, b16 = wide, low_type
+    scratch = [
+        vm((4, 2, 2, UNITS * UNIT, full), b16),
+        vm((16 * UNIT, 256), b16),
+        vm((TOK, full), f32),
+        vm((TOK, full), f32), vm((TOK, full), f32), vm((TOK, full), f32),
+        vm((TOK, full), b16), vm((TOK, full), b16), vm((TOK, full), b16),
+        vm((TOK, 3 * full), b16),
+        vm((4, TOK, full), f32),
+        vm((4, TOK, full), b16),
+        vm((full, vocab), b16),
+        vm((2, full, 256), f32),
+        vm((4, 2, 2, 2 * MSLOT, full), b16),
+        vm((MSLOT, full), b16),
+        vm((2 * MSLOT, full), b16),
+        vm((BANDS, 2 * MSLOT, 512), f32),
+        vm((full, slots), b16),
+        vm((slots, 512), b16),
+        vm((slots, 128), f32),
+        vm((4, 8, 256), f32),
+        vm((16, 8, 256), f32),
+        vm((128, 256), f32),
+        vm((256, 128), f32),
+        vm((2 * MSLOT, full), f32),
+        vm((MSLOT, full), b16), vm((MSLOT, full), b16),
+        vm((TOK, full), b16),
+        vm((TOK, full), f32),
+        vm((8, full), f32),
+        vm((4, 4, 2, UNIT, full), b16),
+        vm((7, 2, 2, UNIT, half), b16),
+        vm((7, 2, UNIT, full), b16),
+        vm((7, 2, UNIT, half), b16),
+        vm((7, 2, UNIT, half), b16),
+        vm((7, 3, UNIT, half), b16),
+        vm((224, full), b16),
+        vm((112, full), b16),
+        vm((5, 112, half), b16),
+        vm((32, 8, 128), f32),
+        dma((UNITS, 12)), dma((UNITS, 12)),
+        dma((16,)), dma((16,)),
+        dma((2, 2)),
+        dma((2, 12)), dma((2, 12)),
+        dma((3,)), dma((3,)),
+        dma((16,)), dma((16,)),
+        dma((UNITS, 8)), dma((UNITS, 8)),
+        dma((6,)), dma((6,)),
+        dma((32,)), dma((32,)),
+        dma((2,)),
+        dma((BANDS,)),
+    ]
+    in_vmem = pl.BlockSpec(memory_space=pltpu.VMEM)
+    return pl.pallas_call(
+        step_kernel,
+        out_shape=(
+            jax.ShapeDtypeStruct((UNITS * UNIT, half), f32),
+            jax.ShapeDtypeStruct((224, half), f32),
+            jax.ShapeDtypeStruct((full, vocab), b16),
+            jax.ShapeDtypeStruct((8, 128), f32),
+        ),
+        in_specs=[
+            in_vmem, in_vmem, in_vmem, in_vmem, in_vmem,
+            pl.BlockSpec(memory_space=pltpu.SMEM),
+            pl.BlockSpec(memory_space=pl.ANY),
+        ],
+        out_specs=(in_vmem, in_vmem, pl.BlockSpec(memory_space=pl.ANY), in_vmem),
+        scratch_shapes=scratch,
+        compiler_params=pltpu.CompilerParams(
+            collective_id=0, has_side_effects=True, vmem_limit_bytes=VMEM_LIMIT
+        ),
+        cost_estimate=pl.CostEstimate(flops=50_000_000_000, bytes_accessed=40_000_000, transcendentals=0),
+    )(pix, blk, tab, places, info, counts, head)
+
+
+def block_path(
+    pixels, mask_places, mask_count, targets, step_count,
+    patch_weight, vector_table, input_weight, output_weight, upward_weight, downward_weight, head_weight,
+    *moments,
+):
+    part = pixels.shape[1]
+    images = pixels.shape[0] // SEQ
+    pix = jnp.transpose(pixels.reshape(images, SEQ, part), (0, 2, 1))
+    pix = jnp.pad(pix, ((0, 0), (0, 0), (0, 256 - SEQ)))
+    up = upward_weight[0].astype(low_type).T
+    blk = jnp.concatenate(
+        [
+            patch_weight.astype(low_type),
+            input_weight[0].astype(low_type).T,
+            output_weight[0].astype(low_type),
+            up,
+            downward_weight[0].astype(low_type),
+        ],
+        axis=0,
+    )
+    tab = jnp.pad(vector_table, ((0, TOK - vector_table.shape[0]), (0, 0)))
+    counted = jnp.arange(MSLOT, dtype=jnp.int32)[None, :] < mask_count[:, None]
+    rows = jnp.stack(
+        [jnp.zeros((2 * MSLOT,), wide), targets.reshape(-1).astype(wide), counted.reshape(-1).astype(wide)]
+    )
+    info = jnp.pad(rows, ((0, 125), (0, 256 - 2 * MSLOT)))
+    gout, gtab, ghead, scal = step_call(pix, blk, tab, mask_places, info, mask_count, head_weight)
+    loss_total, count_total, squares_total = scal[0, 0], scal[1, 0], scal[2, 0]
+    mean_loss = loss_total / count_total
+    grad_norm = jnp.sqrt(squares_total) / count_total
+    factor = jnp.minimum(1.0, clip_limit / grad_norm) / count_total
+    step_value = step_count[0].astype(wide)
+    starts = [0, 1, 4, 5, 9, 13]
+    pieces = [gout[UNIT * starts[n] : UNIT * starts[n + 1]] for n in range(5)]
+    grads = [
+        pieces[0], gtab[: vector_table.shape[0]], pieces[1].T[None], pieces[2][None],
+        pieces[3].T[None], pieces[4][None], ghead.astype(wide),
+    ]
+    weights = [
+        patch_weight, vector_table, input_weight, output_weight, upward_weight, downward_weight, head_weight,
+    ]
+    results = []
+    for n in range(7):
+        results.extend(adam_step(weights[n], grads[n], moments[n], moments[7 + n], factor, step_value))
+    return (mean_loss, grad_norm, *results)
+
+
 def solution(mesh):
     state = (
         P("col", "row"),
@@ -330,8 +1264,9 @@
     )
     data = (P("row", "col"), P("col", None), P("col"), P("col", None), P())
     outs = (P(), P()) + tuple(spec for spec in state for _ in range(3))
+    fits = dict(mesh.shape) == {"row": 2, "col": 16}
     return jax.shard_map(
-        on_device,
+        block_path if fits else on_device,
         mesh=mesh,
         in_specs=data + state * 3,
         out_specs=outs,

time: 814 us -> 305 us (0.37); the launches traced: 804 us -> 305 us
  waiting for transfers between devices: 449 us -> 0 us
  Pallas kernels: 0 us -> 240 us
  local copies, waits for them, and re-layouts: 134 us -> 7.01 us
  blocking collectives: 66.4 us -> 0 us
  matrix products: 58.1 us -> 0 us
  between operations: 26.4 us -> 7.78 us
  starting transfers between devices: 10.8 us -> 0 us
  other arithmetic: 59.5 us -> 49.5 us
    pallas_call x0 -> x1, Pallas kernels: none -> 240 us  [step_call(): pl.pallas_call(step_kernel, out_shape=(jax.ShapeDtypeStruct((UNITS * UNIT...]
    psum x2 -> x0, waiting for transfers between devices: 186 us -> none  [the longest x1 143 us: on_device(): grad_head = lax.psum(grad_head_local.astype(low_type), 'col').astype(wide)]
    reduce_scatter x2 -> x0, waiting for transfers between devices: 176 us -> none  [the longest x1 167 us: on_device(): lax.psum_scatter(stacked, BOTH, scatter_dimension=0, tiled=False)]
    all_gather x1 -> x0, waiting for transfers between devices: 86.4 us -> none  [on_device(): lax.all_gather(jnp.concatenate(blocks, axis=0), BOTH, axis=0, tiled=False)]
    dot_general x25 -> x0, matrix products: 58.1 us -> none  [the longest x5 23.5 us: product_nt(): return jnp.einsum('ab,cb->ac', left, right, preferred_element_type=wide)]
    unnamed x198 -> x28, local copies, waits for them, and re-layouts: 51.5 us -> 0.07 us
    psum x1 -> x0, blocking collectives: 39.5 us -> none  [on_device(): lax.psum((loss_part, count_part, squares_part), BOTH)]
    reshape x7 -> x2, local copies, waits for them, and re-layouts: 33.6 us -> 2.27 us  [block_path(): pix = jnp.transpose(pixels.reshape(images, SEQ, part), (0, 2, 1))]
  transfers between devices with their start and end apart: 7 -> 0, of which waited for: 5 -> 0; matrix products, arithmetic and copies ran while one was open for 14% -> 0% of each run, Pallas kernels for 0% -> 0%
where the time goes in v2:
time: 305 us
  Pallas kernels  240 us (79%)
  other arithmetic  49.5 us (16%)
  between operations  7.78 us (3%)
  local copies, waits for them, and re-layouts  7.01 us (2%)
    pallas_call x1, Pallas kernels, step_call(): pl.pallas_call(step_kernel, out_shape=(jax.ShapeDtypeStruct((UNITS * UNIT...  240 us
    mul x7, other arithmetic, adam_step(): -learn_rate  40.1 us
    unnamed x4, other arithmetic  6.24 us

profile of v2, /device:TPU:0, one launch (start us, length us, event | category | flops | bytes accessed | tf_op | source)
XLA Modules:
  0.0 304.6 jit_solution(3233724472260954202)
XLA Ops:
  0.7 1.5 convert_dynamic-update-slice_fusion
  2.2 1.6 bitcast_dynamic-update-slice_fusion.2
  3.8 1.5 bitcast_dynamic-update-slice_fusion.3
  5.3 1.6 bitcast_dynamic-update-slice_fusion
  6.9 1.6 bitcast_dynamic-update-slice_fusion.1.blk_in
  8.5 2.1 reshape.118
  10.7 0.1 copy.51
  10.8 0.8 pad.12.pix_in
  11.6 1.7 pad.13.tab_in
  13.4 0.7 convert_element_type.75
  14.0 0.1 convert_element_type.76
  14.1 0.7 compare_convert_fusion
  14.8 0.1 reshape.119
  14.9 0.1 pad_maximum_fusion
  15.0 0.7 pad.14.info_in
  15.7 0.0 copy-start.11
  15.7 0.0 copy-start.7
  15.7 0.0 copy-start.12
  15.7 0.0 copy-start.13
  15.7 0.0 copy-start.3
  15.7 0.0 copy-start.8
  15.8 240.3 %shard_map.425 = (f32[624,384]{1,0:T(8,128)}, f32[224,384]{1,0:T(8,128)}, bf16[768,4096]{1,0:T(8,128)(2,1)}, f32[8,128]{1,0:T(8,128)}) custom-call(bf16[16,48,256]{2,1,0:T(8,128)(2,1)} %pad.12.pix_in, bf16[624,384]{1,0:T(8,128)(2,1)} %bitcast_dynamic-update-slice_fusion.1.blk_in, f32[208,384]{1,0:T(8,128)} %pad.13.tab_in, s32[2,80]{1,0:T(2,128)} %places.1, ...), custom_call_target="tpu_custom_call" | custom-call | flops 49999998976 | bytes 40000000 | tf_op jit(solution)/shard_map/pallas_call | solution.py:1186
  256.0 1.3 fusion.18
  260.2 2.0 add_multiply_fusion.2
  262.2 0.0 copy-done.2
  262.2 2.1 add_multiply_fusion.3
  264.3 0.0 copy-done.13
  264.3 1.6 add_multiply_fusion.5
  265.9 2.1 add_multiply_fusion.4
  268.0 1.7 add_multiply_fusion.6
  269.6 29.7 %add_multiply_fusion = (f32[768,4096]{1,0:T(8,128)}, f32[768,4096]{1,0:T(8,128)}, f32[768,4096]{1,0:T(8,128)}) fusion(f32[768,4096]{1,0:T(8,128)} %head_in.1, f32[]{:T(128)} %bitcast.11, f32[]{:T(128)} %bitcast.10, f32[]{:T(128)S(6)} %div.106, bf16[768,4096]{1,0:T(8,128)(2,1)} %get-tuple-element.30, f32[768,4096]{1,0:T(8,128)} %param.51, f32[768,4096]{1,0:T(8,128)} %param.44), kind=kLoop, calls=%fused_computation.2 | loop fusion | flops 50331648 | bytes 81788944 | tf_op jit(solution)/shard_map/mul | solution.py:104
  299.3 1.1 add_multiply_fusion.1
  (21 shorter events, 0.0 us)
Async XLA Ops:
  15.7 244.5 %copy-start.1 = (f32[1,192,384]{2,1,0:T(8,128)S(1)}, f32[1,192,384]{2,1,0:T(8,128)}, u32[]{:S(2)}) copy-start(f32[1,192,384]{2,1,0:T(8,128)} %param.36) | copy-start | bytes 884740
  15.7 244.5 %copy-start.9 = (f32[1,192,384]{2,1,0:T(8,128)S(1)}, f32[1,192,384]{2,1,0:T(8,128)}, u32[]{:S(2)}) copy-start(f32[1,192,384]{2,1,0:T(8,128)} %param.50) | copy-start | bytes 884740
  15.7 244.5 %copy-start.10 = (f32[1,192,384]{2,1,0:T(8,128)S(1)}, f32[1,192,384]{2,1,0:T(8,128)}, u32[]{:S(2)}) copy-start(f32[1,192,384]{2,1,0:T(8,128)} %param.43) | copy-start | bytes 884740
  15.7 246.5 %copy-start.2 = (f32[1,384,192]{1,2,0:T(8,128)S(1)}, f32[1,384,192]{1,2,0:T(8,128)}, u32[]{:S(2)}) copy-start(f32[1,384,192]{1,2,0:T(8,128)} %param.35) | copy-start | bytes 884740
  15.7 246.5 %copy-start.11 = (f32[1,384,192]{1,2,0:T(8,128)S(1)}, f32[1,384,192]{1,2,0:T(8,128)}, u32[]{:S(2)}) copy-start(f32[1,384,192]{1,2,0:T(8,128)} %param.49) | copy-start | bytes 884740
  15.7 248.6 %copy-start.7 = (f32[1,48,384]{2,1,0:T(8,128)S(1)}, f32[1,48,384]{2,1,0:T(8,128)}, u32[]{:S(2)}) copy-start(f32[1,48,384]{2,1,0:T(8,128)} %param.34) | copy-start | bytes 221188
  15.7 248.6 %copy-start.12 = (f32[1,48,384]{2,1,0:T(8,128)S(1)}, f32[1,48,384]{2,1,0:T(8,128)}, u32[]{:S(2)}) copy-start(f32[1,48,384]{2,1,0:T(8,128)} %param.48) | copy-start | bytes 221188
  15.7 248.6 %copy-start.13 = (f32[1,48,384]{2,1,0:T(8,128)S(1)}, f32[1,48,384]{2,1,0:T(8,128)}, u32[]{:S(2)}) copy-start(f32[1,48,384]{2,1,0:T(8,128)} %param.41) | copy-start | bytes 221188
  15.7 250.2 %copy-start.3 = (f32[1,384,144]{1,2,0:T(8,128)S(1)}, f32[1,384,144]{1,2,0:T(8,128)}, u32[]{:S(2)}) copy-start(f32[1,384,144]{1,2,0:T(8,128)} %param.33) | copy-start | bytes 663556
  15.7 252.2 %copy-start.8 = (f32[48,384]{1,0:T(8,128)S(1)}, f32[48,384]{1,0:T(8,128)}, u32[]{:S(2)}) copy-start(f32[48,384]{1,0:T(8,128)} %param.31) | copy-start | bytes 221188
  269.6 29.7 %copy-start = (f32[205,384]{1,0:T(8,128)S(1)}, f32[205,384]{1,0:T(8,128)}, u32[]{:S(2)}) copy-start(f32[205,384]{1,0:T(8,128)} %param.32) | copy-start | bytes 944644
  269.6 29.7 %copy-start.4 = (f32[205,384]{1,0:T(8,128)S(1)}, f32[205,384]{1,0:T(8,128)}, u32[]{:S(2)}) copy-start(f32[205,384]{1,0:T(8,128)} %param.46) | copy-start | bytes 944644
  269.6 29.7 %copy-start.5 = (f32[205,384]{1,0:T(8,128)S(1)}, f32[205,384]{1,0:T(8,128)}, u32[]{:S(2)}) copy-start(f32[205,384]{1,0:T(8,128)} %param.39) | copy-start | bytes 944644
  269.6 29.7 %copy-start.6 = (f32[224,384]{1,0:T(8,128)S(1)}, f32[224,384]{1,0:T(8,128)}, u32[]{:S(2)}) copy-start(f32[224,384]{1,0:T(8,128)} %get-tuple-element.29) | copy-start | bytes 1032196

commit v3 on v2

--- a/solution.py
+++ b/solution.py
@@ -325,6 +325,10 @@
 UNIT = 48
 UNITS = 13
 BANDS = 8
+AHEAD = 4
+LAG_A = 1
+LAG_B = 3
+LAG_C = 4
 EYE = pl.DeviceIdType.MESH
 
 
@@ -369,12 +373,12 @@
 
 
 def step_kernel(
-    pix_in, blk_in, tab_in, places, info_in, counts, head_in,
+    pix_in, patch_in, input_in, output_in, up_in, down_in, tab_in, places, targets, counts, head_in,
     gout, gtab_out, ghead, scal_out,
-    wg, px, tb, st0, st1, st2, n1, n2, mix, qkv, hpre, hact,
+    wg, px_out, px_mid, px, tb, st0, st1, st2, n1, n2, mix, qkv, hpre, hact,
     hn, hbuf, pk, pkp, pp, lt, pkt, gch, colb, sq, lsb, flip, tmpa, gpk, gps, gpr, g2b, gacc, gst,
     rk, r1a, r1b, r2a, r2b, rz, tab, tabk, tabr, fin,
-    ag_send, ag_recv, px_send, px_recv, tb_sem, pk_send, pk_recv, ex_send, ex_recv,
+    ag_send, ag_recv, px_sem, px_send, px_recv, tb_sem, pk_send, pk_recv, ex_send, ex_recv,
     ls_send, ls_recv, rs_send, rs_recv, tab_send, tab_recv, fin_send, fin_recv, hb_sem, gh_sem,
 ):
     r = lax.axis_index("row")
@@ -398,6 +402,7 @@
         return pl.ds(pl.multiple_of(row * half, half), half)
 
     sq[...] = jnp.zeros_like(sq)
+    width = px_out.shape[3]
     barrier = pltpu.get_barrier_semaphore()
 
     def greet(n, _):
@@ -407,9 +412,19 @@
 
     lax.fori_loop(1, 32, greet, 0)
 
-    for n in range(UNITS):
-        wg[z, x, k, UNIT * n : UNIT * (n + 1), lanes(r)] = blk_in[UNIT * n : UNIT * (n + 1)]
-    tb[:, lanes(r)] = tab_in[...]
+    for n in range(16):
+        px_out[n % 2, n // 2, :, 0:SEQ] = pix_in[:, n * SEQ : (n + 1) * SEQ]
+        px_out[n % 2, n // 2, :, SEQ:] = jnp.zeros((UNIT, width - SEQ), low_type)
+    heights = (UNIT, 3 * UNIT, UNIT, 4 * UNIT, 4 * UNIT)
+    blocks = (
+        patch_in[...], input_in[...], output_in[...], up_in[...], down_in[...],
+    )
+    start = 0
+    for height, block in zip(heights, blocks):
+        wg[z, x, k, start : start + height, lanes(r)] = block.astype(low_type)
+        start += height
+    tb[0 : tab_in.shape[0], lanes(r)] = tab_in[...]
+    tb[tab_in.shape[0] :, lanes(r)] = jnp.zeros((TOK - tab_in.shape[0], half), wide)
     hcopy = lambda n: pltpu.make_async_copy(
         head_in.at[:, pl.ds(pl.multiple_of(n * 256, 256), 256)], hbuf.at[n % 2], hb_sem.at[n % 2]
     )
@@ -480,39 +495,47 @@
             (slice(None), cut), pk_send.at[n], pk_recv.at[n],
         )
 
-    def px_move(n):
-        target = (n % 2, 8 * r + n // 2)
-        slot = pl.ds(pl.multiple_of(c * UNIT, UNIT), UNIT)
-        return target, remote(pix_in.at[n], px.at[slot], px_send.at[n], px_recv.at[c], target)
-
-    def px_in(n):
-        slot = pl.ds(pl.multiple_of(n * UNIT, UNIT), UNIT)
-        return remote(px.at[slot], px.at[slot], px_send.at[n], px_recv.at[n], d_y)
-
-    def px_start(n, _):
-        target, copy = px_move(n)
-        mine = jnp.logical_and(target[0] == r, target[1] == c)
-
-        @pl.when(mine)
-        def _():
-            px[pl.ds(pl.multiple_of(c * UNIT, UNIT), UNIT), :] = pix_in[n]
-
-        @pl.when(jnp.logical_not(mine))
-        def _():
-            copy.start()
-
-        return 0
+    px_swap = remote(px_out.at[1 - r], px_mid, px_sem.at[0], px_sem.at[1], d_y)
+
+    def px_slot(n):
+        return px.at[pl.ds(pl.multiple_of(n * UNIT, UNIT), UNIT)]
+
+    def px_move(part, n):
+        target = 8 * (r if part == 0 else 1 - r) + n
+        src = px_out.at[r, n] if part == 0 else px_mid.at[n]
+        return target, remote(src, px_slot(c), px_send.at[part, n], px_recv.at[c], (r, target))
+
+    def px_start(part):
+        def one(n, _):
+            target, copy = px_move(part, n)
+
+            @pl.when(target == c)
+            def _():
+                px[pl.ds(pl.multiple_of(c * UNIT, UNIT), UNIT), :] = (
+                    px_out[r, n] if part == 0 else px_mid[n]
+                )
+
+            @pl.when(target != c)
+            def _():
+                copy.start()
+
+            return 0
+
+        lax.fori_loop(0, 8, one, 0)
 
     def px_done(n, _):
-        target, copy = px_move(n)
-
-        @pl.when(jnp.logical_not(jnp.logical_and(target[0] == r, target[1] == c)))
-        def _():
-            copy.wait_send()
-
-        @pl.when(jnp.logical_not(jnp.logical_and(n == c, r == c // 8)))
-        def _():
-            px_in(n).wait_recv()
+        for part in range(2):
+            target, copy = px_move(part, n)
+
+            @pl.when(target != c)
+            def _():
+                copy.wait_send()
+
+        for source in (n, n + 8):
+
+            @pl.when(source != c)
+            def _():
+                remote(px_slot(source), px_slot(source), px_send.at[0, n], px_recv.at[source], d_y).wait_recv()
 
         return 0
 
@@ -573,7 +596,7 @@
     def do_patch():
         tb_copy(own_cut, 1 - r, 0, d_y).wait_recv()
         tb_copy(own_cut, 1 - r, 1, d_k).start()
-        lax.fori_loop(0, 16, px_done, 0)
+        lax.fori_loop(0, 8, px_done, 0)
         patch = tn(px[...], square(0))[:TOK]
         tb_copy(own_cut, r, 0, d_y).wait_send()
         tb_copy(other_cut, 1 - r, 1, d_k).wait_recv()
@@ -611,38 +634,47 @@
     def do_down(j):
         st2[...] += nn(hact[j], square(9 + j))
 
+    px_swap.start()
     begin(weight_moves(0)[0])
-    lax.fori_loop(0, 16, px_start, 0)
+    begin(weight_moves(1)[0])
+    px_start(0)
+    for n in range(2, AHEAD):
+        begin(weight_moves(n)[0])
     tb_copy(own_cut, r, 0, d_y).start()
 
     def tick(t, _):
-        @pl.when(jnp.logical_and(t >= 1, t < UNITS))
-        def _():
-            begin(weight_moves(t)[0])
-
-        @pl.when(jnp.logical_and(t >= 2, t < UNITS + 2))
-        def _():
-            first, second, pair_one, _, _, _ = weight_moves(t - 2)
+        @pl.when(t < UNITS)
+        def _():
+            first, second, pair_one, _, _, _ = weight_moves(t)
             landed(first)
             begin(second)
             begin(pair_one)
 
-        @pl.when(jnp.logical_and(t >= 3, t < UNITS + 3))
-        def _():
-            _, second, _, third, pair_two, _ = weight_moves(t - 3)
+        @pl.when(t == 0)
+        def _():
+            px_swap.wait()
+            px_start(1)
+
+        @pl.when(t < UNITS - AHEAD)
+        def _():
+            begin(weight_moves(t + AHEAD)[0])
+
+        @pl.when(jnp.logical_and(t >= LAG_A, t < UNITS + LAG_A))
+        def _():
+            _, second, _, third, pair_two, _ = weight_moves(t - LAG_A)
             landed(second)
             begin(third)
             begin(pair_two)
 
-        @pl.when(jnp.logical_and(t >= 5, t < UNITS + 5))
-        def _():
-            _, _, _, third, _, pair_three = weight_moves(t - 5)
+        @pl.when(jnp.logical_and(t >= LAG_B, t < UNITS + LAG_B))
+        def _():
+            _, _, _, third, _, pair_three = weight_moves(t - LAG_B)
             landed(third)
             begin(pair_three)
 
-        @pl.when(t >= 6)
-        def _():
-            _, _, pair_one, _, pair_two, pair_three = weight_moves(t - 6)
+        @pl.when(t >= LAG_C)
+        def _():
+            _, _, pair_one, _, pair_two, pair_three = weight_moves(t - LAG_C)
             landed(pair_one)
             landed(pair_two)
             landed(pair_three)
@@ -656,29 +688,29 @@
             hcopy(t).wait()
             hn[:, pl.ds(pl.multiple_of(t * 256, 256), 256)] = hbuf[t % 2].astype(low_type)
 
-        @pl.when(t == 6)
+        @pl.when(t == LAG_C + 2)
         def _():
             do_patch()
 
-        @pl.when(t == 9)
+        @pl.when(t == LAG_C + 3)
         def _():
             do_attention()
 
-        @pl.when(t == 10)
+        @pl.when(t == LAG_C + 4)
         def _():
             do_output()
 
-        @pl.when(jnp.logical_and(t >= 11, t < 15))
-        def _():
-            do_up(t - 11)
-
-        @pl.when(t >= 15)
-        def _():
-            do_down(t - 15)
+        @pl.when(jnp.logical_and(t >= LAG_C + 5, t < LAG_C + 9))
+        def _():
+            do_up(t - LAG_C - 5)
+
+        @pl.when(t >= LAG_C + 9)
+        def _():
+            do_down(t - LAG_C - 9)
 
         return 0
 
-    lax.fori_loop(0, UNITS + 6, tick, 0)
+    lax.fori_loop(0, UNITS + LAG_C, tick, 0)
 
     def all_sent(n, _):
         for moves in weight_moves(n):
@@ -700,9 +732,14 @@
     for n in range(2):
         begin(picked_moves(n)[0])
     lax.fori_loop(0, UNITS, all_sent, 0)
-    info = jnp.transpose(info_in[...])
-    target_col = info[: 2 * MSLOT, 1:2]
-    weight_col = info[: 2 * MSLOT, 2:3]
+    flip[...] = jnp.zeros_like(flip)
+    flip[0:2, 0:MSLOT] = targets[...].astype(wide)
+    info = jnp.transpose(flip[...])
+    target_col = jnp.concatenate([info[:MSLOT, 0:1], info[:MSLOT, 1:2]], axis=0)
+    slot_line = lax.broadcasted_iota(jnp.int32, (MSLOT, 1), 0)
+    weight_col = jnp.concatenate(
+        [jnp.where(slot_line < counts[0], 1.0, 0.0), jnp.where(slot_line < counts[1], 1.0, 0.0)], axis=0
+    )
     base = (r * (BANDS * 512)).astype(wide)
     band_lane = lax.broadcasted_iota(jnp.int32, (1, 512), 1).astype(wide)
 
@@ -1022,65 +1059,64 @@
         lax.fori_loop(0, 4, turn, 0)
 
     def back_step(s, _):
-        @pl.when(s < 4)
-        def _():
-            back_down(3 - s)
-
-        @pl.when(jnp.logical_and(s >= 4, s < 8))
-        def _():
-            back_up(7 - s)
-
-        @pl.when(s == 8)
-        def _():
-            back_output()
-
-        @pl.when(s == 9)
-        def _():
-            back_attention()
-
-        @pl.when(s == 12)
-        def _():
-            back_patch()
+        def work(q, _):
+            w = jnp.where(s <= 4, 2 * s - 1 + q, s + 4 + 6 * q)
+
+            @pl.when(jnp.logical_and(w >= 0, w < 4))
+            def _():
+                back_down(3 - w)
+
+            @pl.when(jnp.logical_and(w >= 4, w < 8))
+            def _():
+                back_up(7 - w)
+
+            @pl.when(w == 8)
+            def _():
+                back_output()
+
+            @pl.when(w == 9)
+            def _():
+                back_attention()
+
+            @pl.when(w == 10)
+            def _():
+                back_patch()
+
+            return 0
+
+        lax.fori_loop(0, 2, work, 0)
+
+        @pl.when(s < UNITS)
+        def _():
+            sum_start(sums_moves(s)[0])
+
+        @pl.when(jnp.logical_and(s >= 1, s < UNITS + 1))
+        def _():
+            sums_one(s - 1)
+
+        @pl.when(jnp.logical_and(s >= 3, s < UNITS + 3))
+        def _():
+            sums_two(s - 3)
+
+        @pl.when(jnp.logical_and(s >= 5, s < UNITS + 5))
+        def _():
+            sums_three(s - 5)
+
+        @pl.when(s >= 7)
+        def _():
+            sums_four(s - 7)
+
+        @pl.when(s == 6)
+        def _():
             tab_moves[0].start()
-
-        @pl.when(s < UNITS)
-        def _():
-            sum_start(sums_moves(s)[0])
-
-        @pl.when(jnp.logical_and(s >= 1, s < UNITS + 1))
-        def _():
-            sums_one(s - 1)
-
-        @pl.when(jnp.logical_and(s >= 3, s < UNITS + 3))
-        def _():
-            sums_two(s - 3)
-
-        @pl.when(jnp.logical_and(s >= 5, s < UNITS + 5))
-        def _():
-            sums_three(s - 5)
-
-        @pl.when(s >= 7)
-        def _():
-            sums_four(s - 7)
+            head_ready()
 
         for n in range(6):
-            @pl.when(s == 13 + n)
+            @pl.when(s == 7 + 2 * n)
             def _():
                 tab_step(n)
 
-        @pl.when(s == 2)
-        def _():
-            head_ready()
-
-        @pl.when(jnp.logical_and(s >= 3, s < 7))
-        def _():
-            head_band(s - 3)
-
-        @pl.when(jnp.logical_and(s >= 10, s < 12))
-        def _():
-            head_band(s - 6)
-
-        @pl.when(jnp.logical_and(s >= 13, s < 15))
+        @pl.when(jnp.logical_and(s >= 7, s < 15))
         def _():
             head_band(s - 7)
 
@@ -1122,10 +1158,16 @@
     for v in range(BANDS):
         gh_copy(v).wait()
     lax.fori_loop(1, 32, fin_done, 0)
-    scal_out[...] = jnp.sum(fin[...], axis=0)
-
-
-def step_call(pix, blk, tab, places, info, counts, head):
+    totals = jnp.sum(fin[...], axis=0)
+    count_total = totals[1:2, :]
+    norm_value = jnp.sqrt(totals[2:3, :]) / count_total
+    scal_out[0:1, :] = totals[0:1, :] / count_total
+    scal_out[1:2, :] = norm_value
+    scal_out[2:3, :] = jnp.minimum(1.0, clip_limit / norm_value) / count_total
+    scal_out[3:8, :] = jnp.zeros((5, 128), wide)
+
+
+def step_call(pix, blocks, tab, places, targets, counts, head):
     half = tab.shape[1]
     full = 2 * half
     vocab = head.shape[1]
@@ -1135,6 +1177,8 @@
     f32, b16 = wide, low_type
     scratch = [
         vm((4, 2, 2, UNITS * UNIT, full), b16),
+        vm((2, 8, UNIT, 256), b16),
+        vm((8, UNIT, 256), b16),
         vm((16 * UNIT, 256), b16),
         vm((TOK, full), f32),
         vm((TOK, full), f32), vm((TOK, full), f32), vm((TOK, full), f32),
@@ -1171,7 +1215,7 @@
         vm((5, 112, half), b16),
         vm((32, 8, 128), f32),
         dma((UNITS, 12)), dma((UNITS, 12)),
-        dma((16,)), dma((16,)),
+        dma((2,)), dma((2, 8)), dma((16,)),
         dma((2, 2)),
         dma((2, 12)), dma((2, 12)),
         dma((3,)), dma((3,)),
@@ -1192,7 +1236,7 @@
             jax.ShapeDtypeStruct((8, 128), f32),
         ),
         in_specs=[
-            in_vmem, in_vmem, in_vmem, in_vmem, in_vmem,
+            *([in_vmem] * 9),
             pl.BlockSpec(memory_space=pltpu.SMEM),
             pl.BlockSpec(memory_space=pl.ANY),
         ],
@@ -1202,7 +1246,7 @@
             collective_id=0, has_side_effects=True, vmem_limit_bytes=VMEM_LIMIT
         ),
         cost_estimate=pl.CostEstimate(flops=50_000_000_000, bytes_accessed=40_000_000, transcendentals=0),
-    )(pix, blk, tab, places, info, counts, head)
+    )(pix, *blocks, tab, places, targets, counts, head)
 
 
 def block_path(
@@ -1210,46 +1254,192 @@
     patch_weight, vector_table, input_weight, output_weight, upward_weight, downward_weight, head_weight,
     *moments,
 ):
-    part = pixels.shape[1]
-    images = pixels.shape[0] // SEQ
-    pix = jnp.transpose(pixels.reshape(images, SEQ, part), (0, 2, 1))
-    pix = jnp.pad(pix, ((0, 0), (0, 0), (0, 256 - SEQ)))
-    up = upward_weight[0].astype(low_type).T
-    blk = jnp.concatenate(
-        [
-            patch_weight.astype(low_type),
-            input_weight[0].astype(low_type).T,
-            output_weight[0].astype(low_type),
-            up,
-            downward_weight[0].astype(low_type),
+    weights = (
+        patch_weight, vector_table, input_weight, output_weight, upward_weight, downward_weight, head_weight,
+    )
+    weights = flat(weights)
+    blocks = [weights[n] for n in (0, 2, 3, 4, 5)]
+    gout, gtab, ghead, scal = step_call(
+        pixels.T, blocks, vector_table, mask_places, targets, mask_count, head_weight
+    )
+    results = adam_call(
+        scal, step_count, gout, gtab, ghead, weights, flat(moments[:7]), flat(moments[7:])
+    )
+    triples = [results[2 + n :: 3] for n in range(3)]
+    triples = [unflat(triple) for triple in triples]
+    return (*results[:2], *(triple[n] for n in range(7) for triple in triples))
+
+
+def flat(values):
+    patch, table, inward, outward, up, down, head = values
+    return (patch, table, inward[0].T, outward[0], up[0].T, down[0], head)
+
+
+def unflat(values):
+    patch, table, inward, outward, up, down, head = values
+    return (patch, table, inward.T[None], outward[None], up.T[None], down[None], head)
+
+
+SMALL = UNITS * UNIT
+ROWS = 48
+IN_SLOTS = 4
+OUT_SLOTS = 3
+
+
+def adam_kernel(
+    scal, step, gout, gtab, ghead, *refs
+):
+    weights, drifts, powers = refs[:7], refs[7:14], refs[14:21]
+    loss_out, norm_out = refs[21:23]
+    outs = refs[23:44]
+    gbuf, inbuf, outbuf, gsm, insm, outsm, gtb, intb, outtb, in_sem, out_sem, sm_in, sm_out = refs[44:]
+    factor = scal[2:3, 0:1]
+    count = jnp.full((1, 128), step[0], jnp.int32).astype(wide)[:, 0:1]
+    scale_first = 1.0 / (1.0 - jnp.exp(count * math.log(beta_first)))
+    scale_second = 1.0 / (1.0 - jnp.exp(count * math.log(beta_second)))
+    count_first = scale_first * -learn_rate
+    gain_first = factor * (1.0 - beta_first)
+    gain_second = factor * factor * (1.0 - beta_second)
+    chunks = ghead.shape[0] // ROWS
+    states = (weights, drifts, powers)
+
+    def rows_of(n):
+        return pl.ds(pl.multiple_of(n * ROWS, ROWS), ROWS)
+
+    def fetch(n):
+        slot = lax.rem(n, IN_SLOTS)
+        copies = [
+            pltpu.make_async_copy(states[m][6].at[rows_of(n)], inbuf.at[slot, m], in_sem.at[slot, m])
+            for m in range(3)
+        ]
+        copies.append(pltpu.make_async_copy(ghead.at[rows_of(n)], gbuf.at[slot], in_sem.at[slot, 3]))
+        return copies
+
+    def store(n):
+        slot = lax.rem(n, OUT_SLOTS)
+        return [
+            pltpu.make_async_copy(outbuf.at[slot, m], outs[18 + m].at[rows_of(n)], out_sem.at[slot, m])
+            for m in range(3)
+        ]
+
+    order = (0, 2, 3, 4, 5)
+    small_fetch, small_store = [], []
+    start = 0
+    for at, n in enumerate(order):
+        height = weights[n].shape[0]
+        for m in range(3):
+            small_fetch.append(
+                pltpu.make_async_copy(states[m][n], insm.at[m, start : start + height], sm_in.at[at, m])
+            )
+            small_store.append(
+                pltpu.make_async_copy(outsm.at[m, start : start + height], outs[3 * n + m], sm_out.at[at, m])
+            )
+        start += height
+    for m in range(3):
+        small_fetch.append(pltpu.make_async_copy(states[m][1], intb.at[m], sm_in.at[5, m]))
+        small_store.append(pltpu.make_async_copy(outtb.at[m], outs[3 + m], sm_out.at[5, m]))
+    small_fetch.append(pltpu.make_async_copy(gout, gsm, sm_in.at[6, 0]))
+    small_fetch.append(pltpu.make_async_copy(gtab, gtb, sm_in.at[6, 1]))
+
+    def adam(grad, weight, drift, power):
+        new_drift = beta_first * drift + gain_first * grad
+        new_power = beta_second * power + gain_second * (grad * grad)
+        below = jnp.sqrt(new_power * scale_second) + adam_eps
+        update = new_drift * count_first / below - (learn_rate * weight_decay) * weight
+        return update, new_drift, new_power
+
+    for n in range(IN_SLOTS):
+        for copy in fetch(n):
+            copy.start()
+    for copy in small_fetch:
+        copy.start()
+    loss_out[...] = scal[0:1, 0:1]
+    norm_out[...] = scal[1:2, 0:1]
+
+    def chunk(n, _):
+        for copy in fetch(n):
+            copy.wait()
+
+        @pl.when(n >= OUT_SLOTS)
+        def _():
+            for copy in store(n - OUT_SLOTS):
+                copy.wait()
+
+        slot, spot = lax.rem(n, IN_SLOTS), lax.rem(n, OUT_SLOTS)
+
+        def part(q, _):
+            at = pl.ds(pl.multiple_of(q * 16, 16), 16)
+            values = adam(
+                gbuf[slot, at, :].astype(wide), inbuf[slot, 0, at, :], inbuf[slot, 1, at, :],
+                inbuf[slot, 2, at, :],
+            )
+            for m in range(3):
+                outbuf[spot, m, at, :] = values[m]
+            return 0
+
+        lax.fori_loop(0, ROWS // 16, part, 0)
+        for copy in store(n):
+            copy.start()
+
+        @pl.when(n + IN_SLOTS < chunks)
+        def _():
+            for copy in fetch(n + IN_SLOTS):
+                copy.start()
+
+        @pl.when(n == 2)
+        def _():
+            for copy in small_fetch:
+                copy.wait()
+
+            def small(q, _):
+                at = pl.ds(pl.multiple_of(q * UNIT, UNIT), UNIT)
+                values = adam(gsm[at, :], insm[0, at, :], insm[1, at, :], insm[2, at, :])
+                for m in range(3):
+                    outsm[m, at, :] = values[m]
+                return 0
+
+            lax.fori_loop(0, UNITS, small, 0)
+            values = adam(gtb[0 : intb.shape[1]], intb[0], intb[1], intb[2])
+            for m in range(3):
+                outtb[m] = values[m]
+            for copy in small_store:
+                copy.start()
+
+        return 0
+
+    lax.fori_loop(0, chunks, chunk, 0)
+    for n in range(chunks - OUT_SLOTS, chunks):
+        for copy in store(n):
+            copy.wait()
+    for copy in small_store:
+        copy.wait()
+
+
+def adam_call(scal, step, gout, gtab, ghead, weights, drifts, powers):
+    half = gout.shape[1]
+    vocab = ghead.shape[1]
+    table = weights[1].shape[0]
+    one = jax.ShapeDtypeStruct((1, 1), wide)
+    shapes = [jax.ShapeDtypeStruct(value.shape, wide) for value in weights for _ in range(3)]
+    in_vmem = pl.BlockSpec(memory_space=pltpu.VMEM)
+    anywhere = pl.BlockSpec(memory_space=pl.ANY)
+    vm, dma = pltpu.VMEM, pltpu.SemaphoreType.DMA
+    results = pl.pallas_call(
+        adam_kernel,
+        in_specs=[in_vmem, pl.BlockSpec(memory_space=pltpu.SMEM)] + [anywhere] * 24,
+        out_specs=[in_vmem] * 2 + [anywhere] * 21,
+        out_shape=[one, one] + shapes,
+        scratch_shapes=[
+            vm((IN_SLOTS, ROWS, vocab), low_type), vm((IN_SLOTS, 3, ROWS, vocab), wide),
+            vm((OUT_SLOTS, 3, ROWS, vocab), wide),
+            vm((SMALL, half), wide), vm((3, SMALL, half), wide), vm((3, SMALL, half), wide),
+            vm(gtab.shape, wide), vm((3, table, half), wide), vm((3, table, half), wide),
+            dma((IN_SLOTS, 4)), dma((OUT_SLOTS, 3)), dma((7, 3)), dma((6, 3)),
         ],
-        axis=0,
-    )
-    tab = jnp.pad(vector_table, ((0, TOK - vector_table.shape[0]), (0, 0)))
-    counted = jnp.arange(MSLOT, dtype=jnp.int32)[None, :] < mask_count[:, None]
-    rows = jnp.stack(
-        [jnp.zeros((2 * MSLOT,), wide), targets.reshape(-1).astype(wide), counted.reshape(-1).astype(wide)]
-    )
-    info = jnp.pad(rows, ((0, 125), (0, 256 - 2 * MSLOT)))
-    gout, gtab, ghead, scal = step_call(pix, blk, tab, mask_places, info, mask_count, head_weight)
-    loss_total, count_total, squares_total = scal[0, 0], scal[1, 0], scal[2, 0]
-    mean_loss = loss_total / count_total
-    grad_norm = jnp.sqrt(squares_total) / count_total
-    factor = jnp.minimum(1.0, clip_limit / grad_norm) / count_total
-    step_value = step_count[0].astype(wide)
-    starts = [0, 1, 4, 5, 9, 13]
-    pieces = [gout[UNIT * starts[n] : UNIT * starts[n + 1]] for n in range(5)]
-    grads = [
-        pieces[0], gtab[: vector_table.shape[0]], pieces[1].T[None], pieces[2][None],
-        pieces[3].T[None], pieces[4][None], ghead.astype(wide),
-    ]
-    weights = [
-        patch_weight, vector_table, input_weight, output_weight, upward_weight, downward_weight, head_weight,
-    ]
-    results = []
-    for n in range(7):
-        results.extend(adam_step(weights[n], grads[n], moments[n], moments[7 + n], factor, step_value))
-    return (mean_loss, grad_norm, *results)
+        compiler_params=pltpu.CompilerParams(vmem_limit_bytes=VMEM_LIMIT),
+        cost_estimate=pl.CostEstimate(flops=60_000_000, bytes_accessed=82_000_000, transcendentals=4_000_000),
+    )(scal, step, gout, gtab, ghead, *weights, *drifts, *powers)
+    return (results[0].reshape(()), results[1].reshape(()), *results[2:])
 
 
 def solution(mesh):

time: 305 us -> 259 us (0.85)
  other arithmetic: 49.5 us -> 0 us
  Pallas kernels: 240 us -> 258 us
  local copies, waits for them, and re-layouts: 7.01 us -> 0 us
  between operations: 7.78 us -> 1.47 us
    mul x7 -> x0, other arithmetic: 40.1 us -> none  [adam_step(): -learn_rate]
    pallas_call x0 -> x1, Pallas kernels: none -> 32.4 us  [adam_call(): pl.pallas_call(adam_kernel, in_specs=[in_vmem, pl.BlockSpec(memory_space=...]
    pallas_call x1, Pallas kernels: 240 us -> 225 us  [step_call(): pl.pallas_call(step_kernel, out_shape=(jax.ShapeDtypeStruct((UNITS * UNIT...]
    unnamed x4 -> x0, other arithmetic: 6.24 us -> none
    pad x3 -> x0, local copies, waits for them, and re-layouts: 3.19 us -> none  [the longest x1 1.71 us: block_path(): tab = jnp.pad(vector_table, ((0, TOK - vector_table.shape[0]), (0, 0)))]
where the time goes in v3:
time: 259 us
  Pallas kernels  258 us (100%)
    pallas_call x1, Pallas kernels, step_call(): pl.pallas_call(step_kernel, out_shape=(jax.ShapeDtypeStruct((UNITS * UNIT...  225 us
    pallas_call x1, Pallas kernels, adam_call(): pl.pallas_call(adam_kernel, in_specs=[in_vmem, pl.BlockSpec(memory_space=...  32.4 us

profile of v3, /device:TPU:0, one launch (start us, length us, event | category | flops | bytes accessed | tf_op | source)
XLA Modules:
  0.0 259.2 jit_solution(16522447670072386154)
XLA Ops:
  1.3 225.4 %shard_map.425 = (f32[624,384]{1,0:T(8,128)}, f32[224,384]{1,0:T(8,128)}, bf16[768,4096]{1,0:T(8,128)(2,1)}, f32[8,128]{1,0:T(8,128)}) custom-call(bf16[48,3152]{1,0:T(8,128)(2,1)} %bitcast.67, f32[48,384]{1,0:T(8,128)} %refs_0_.1, f32[144,384]{1,0:T(8,128)} %bitcast.59, f32[48,384]{1,0:T(8,128)} %bitcast.63, f32[192,384]{1,0:T(8,128)} %bitcast.51, ...), custom_call_target="tpu_custom_call" | custom-call | flops 49999998976 | bytes 40000000 | tf_op jit(solution)/shard_map/pallas_call | solution.py:1230
  226.7 32.4 %shard_map.426 = (f32[1,1]{1,0:T(1,128)}, f32[1,1]{1,0:T(1,128)}, f32[48,384]{1,0:T(8,128)}, f32[48,384]{1,0:T(8,128)}, f32[48,384]{1,0:T(8,128)}, /*index=5*/f3...) custom-call(f32[8,128]{1,0:T(8,128)} %get-tuple-element.50.scal, ...), custom_call_target="tpu_custom_call" | custom-call | flops 60000000 | bytes 82000000 | tf_op jit(solution)/shard_map/pallas_call | solution.py:1427

commit v4 on v3

--- a/solution.py
+++ b/solution.py
@@ -325,6 +325,7 @@
 UNIT = 48
 UNITS = 13
 BANDS = 8
+G_FIRST = 7
 AHEAD = 4
 LAG_A = 1
 LAG_B = 3
@@ -379,7 +380,7 @@
     hn, hbuf, pk, pkp, pp, lt, pkt, gch, colb, sq, lsb, flip, tmpa, gpk, gps, gpr, g2b, gacc, gst,
     rk, r1a, r1b, r2a, r2b, rz, tab, tabk, tabr, fin,
     ag_send, ag_recv, px_sem, px_send, px_recv, tb_sem, pk_send, pk_recv, ex_send, ex_recv,
-    ls_send, ls_recv, rs_send, rs_recv, tab_send, tab_recv, fin_send, fin_recv, hb_sem, gh_sem,
+    ls_send, ls_recv, rs_send, rs_recv, tab_send, tab_recv, fin_send, fin_recv, hb_sem, gh_sem, gh_send, gh_recv,
 ):
     r = lax.axis_index("row")
     c = lax.axis_index("col")
@@ -488,6 +489,26 @@
             wg, lambda row: (rows, lanes(row)), (rows, slice(None)), ag_send.at[n], ag_recv.at[n]
         )
 
+    late = UNITS - 1
+
+    def late_moves():
+        rows = unit_rows(late)
+        every = slice(None)
+
+        def move(index, out_region, in_region, device):
+            out_ref, in_ref = wg.at[out_region], wg.at[in_region]
+            send, recv = ag_send.at[late, index], ag_recv.at[late, index]
+            return remote(out_ref, out_ref, send, recv, device), remote(in_ref, in_ref, send, recv, device)
+
+        one = [move(0, (z, x, k, rows, lanes(r)), (z, 1 - x, k, rows, lanes(r)), d_x)]
+        two = [move(1, (z, every, k, rows, lanes(r)), (z, every, k, rows, lanes(1 - r)), d_y)]
+        three = [
+            move(1 + n, (z, every, k, rows, every), (lax.rem(z + 4 - n, 4), every, k, rows, every), d_z(n))
+            for n in (1, 2, 3)
+        ]
+        four = [move(5, (every, every, k, rows, every), (every, every, 1 - k, rows, every), d_k)]
+        return one, two, three, four
+
     def picked_moves(n):
         cut = lanes(n)
         return gather_moves(
@@ -634,6 +655,7 @@
     def do_down(j):
         st2[...] += nn(hact[j], square(9 + j))
 
+    begin(late_moves()[0])
     px_swap.start()
     begin(weight_moves(0)[0])
     begin(weight_moves(1)[0])
@@ -643,7 +665,7 @@
     tb_copy(own_cut, r, 0, d_y).start()
 
     def tick(t, _):
-        @pl.when(t < UNITS)
+        @pl.when(t < late)
         def _():
             first, second, pair_one, _, _, _ = weight_moves(t)
             landed(first)
@@ -652,32 +674,48 @@
 
         @pl.when(t == 0)
         def _():
+            landed(late_moves()[0])
+            begin(late_moves()[1])
             px_swap.wait()
             px_start(1)
 
-        @pl.when(t < UNITS - AHEAD)
+        @pl.when(t < late - AHEAD)
         def _():
             begin(weight_moves(t + AHEAD)[0])
 
-        @pl.when(jnp.logical_and(t >= LAG_A, t < UNITS + LAG_A))
+        @pl.when(t == late - AHEAD)
+        def _():
+            landed(late_moves()[1])
+            begin(late_moves()[2])
+
+        @pl.when(jnp.logical_and(t >= LAG_A, t < late + LAG_A))
         def _():
             _, second, _, third, pair_two, _ = weight_moves(t - LAG_A)
             landed(second)
             begin(third)
             begin(pair_two)
 
-        @pl.when(jnp.logical_and(t >= LAG_B, t < UNITS + LAG_B))
+        @pl.when(t == late + 2)
+        def _():
+            landed(late_moves()[2])
+            begin(late_moves()[3])
+
+        @pl.when(jnp.logical_and(t >= LAG_B, t < late + LAG_B))
         def _():
             _, _, _, third, _, pair_three = weight_moves(t - LAG_B)
             landed(third)
             begin(pair_three)
 
-        @pl.when(t >= LAG_C)
+        @pl.when(jnp.logical_and(t >= LAG_C, t < late + LAG_C))
         def _():
             _, _, pair_one, _, pair_two, pair_three = weight_moves(t - LAG_C)
             landed(pair_one)
             landed(pair_two)
             landed(pair_three)
+
+        @pl.when(t == late + LAG_C)
+        def _():
+            landed(late_moves()[3])
 
         @pl.when(t < 2 * BANDS)
         def _():
@@ -731,7 +769,9 @@
     swap_picked.start()
     for n in range(2):
         begin(picked_moves(n)[0])
-    lax.fori_loop(0, UNITS, all_sent, 0)
+    lax.fori_loop(0, late, all_sent, 0)
+    for moves in late_moves():
+        sent(moves)
     flip[...] = jnp.zeros_like(flip)
     flip[0:2, 0:MSLOT] = targets[...].astype(wide)
     info = jnp.transpose(flip[...])
@@ -1021,23 +1061,33 @@
         if n < 5:
             tab_moves[n + 1].start()
 
-    def gh_copy(v):
-        return pltpu.make_async_copy(hn.at[:, band(v)], ghead.at[:, band(v)], gh_sem.at[v])
-
-    def head_band(v):
-        def rows_block(n, _):
-            at = pl.ds(pl.multiple_of(n * 4 * MSLOT, 16), 4 * MSLOT)
-            value = nn(pk[n // 2, n % 2].reshape(4 * MSLOT, 2 * half), hn[:, band(v)])
+    def gh_moves(n):
+        own, other = band(k * (BANDS // 2) + n), band((1 - k) * (BANDS // 2) + n)
+        keep = pltpu.make_async_copy(hn.at[:, own], ghead.at[:, own], gh_sem.at[n])
+        give = remote(hn.at[:, own], ghead.at[:, own], gh_send.at[n], gh_recv.at[n], d_k)
+        take = remote(hn.at[:, other], ghead.at[:, other], gh_send.at[n], gh_recv.at[n], d_k)
+        return keep, give, take
+
+    def head_logits(n):
+        v = k * (BANDS // 2) + n
+
+        def rows_block(m, _):
+            at = pl.ds(pl.multiple_of(m * 8 * MSLOT, 128), 8 * MSLOT)
+            value = nn(pk[m].reshape(8 * MSLOT, 2 * half), hn[:, band(v)])
             cols = colb[at, :]
             hit = jnp.where(band_hit(v, cols[:, 1:2]), 1.0, 0.0)
             gch[at, :] = ((jnp.exp(value - cols[:, 0:1]) - hit) * cols[:, 2:3]).astype(low_type)
             return 0
 
-        lax.fori_loop(0, 8, rows_block, 0)
+        lax.fori_loop(0, 4, rows_block, 0)
+
+    def head_grad(n):
         value = nn(pkt[...], gch[...])
         sq[3, 0:1, 0:128] += jnp.sum(jnp.sum(value * value, axis=0, keepdims=True), axis=1, keepdims=True)
-        hn[:, band(v)] = value.astype(low_type)
-        gh_copy(v).start()
+        hn[:, band(k * (BANDS // 2) + n)] = value.astype(low_type)
+        keep, give, _ = gh_moves(n)
+        keep.start()
+        give.start()
 
     def head_ready():
         for n in range(2):
@@ -1106,19 +1156,28 @@
         def _():
             sums_four(s - 7)
 
+        @pl.when(s == 2)
+        def _():
+            head_ready()
+
         @pl.when(s == 6)
         def _():
             tab_moves[0].start()
-            head_ready()
 
         for n in range(6):
             @pl.when(s == 7 + 2 * n)
             def _():
                 tab_step(n)
 
-        @pl.when(jnp.logical_and(s >= 7, s < 15))
-        def _():
-            head_band(s - 7)
+        @pl.when(jnp.logical_and(s >= G_FIRST, s < G_FIRST + BANDS))
+        def _():
+            @pl.when((s - G_FIRST) % 2 == 0)
+            def _():
+                head_logits((s - G_FIRST) // 2)
+
+            @pl.when((s - G_FIRST) % 2 == 1)
+            def _():
+                head_grad((s - G_FIRST) // 2)
 
         return 0
 
@@ -1127,9 +1186,10 @@
     gtab_out[rows_other, :] = tabr[4].astype(wide)
     value = gtab_out[...]
     first_col = jnp.where(c == 0, 1.0, 0.0)
+    first_chip = jnp.where(c < 2, 1.0, 0.0)
     table_squares = jnp.sum(jnp.sum(value * value, axis=0, keepdims=True), axis=1, keepdims=True)
     line = lax.broadcasted_iota(jnp.int32, (8, 128), 0)
-    squares = sq[2, 0:1, 0:128] + (sq[3, 0:1, 0:128] + table_squares) * first_col
+    squares = sq[2, 0:1, 0:128] + sq[3, 0:1, 0:128] * first_chip + table_squares * first_col
     count = (counts[0] + counts[1]).astype(wide) * leader
     fin[r * 16 + c] = jnp.where(
         line == 0, loss_part, jnp.where(line == 1, count, jnp.where(line == 2, squares, 0.0))
@@ -1155,8 +1215,11 @@
     for n in range(2):
         for moves in picked_moves(n):
             sent(moves)
-    for v in range(BANDS):
-        gh_copy(v).wait()
+    for n in range(BANDS // 2):
+        keep, give, take = gh_moves(n)
+        keep.wait()
+        give.wait_send()
+        take.wait_recv()
     lax.fori_loop(1, 32, fin_done, 0)
     totals = jnp.sum(fin[...], axis=0)
     count_total = totals[1:2, :]
@@ -1224,7 +1287,7 @@
         dma((6,)), dma((6,)),
         dma((32,)), dma((32,)),
         dma((2,)),
-        dma((BANDS,)),
+        dma((BANDS // 2,)), dma((BANDS // 2,)), dma((BANDS // 2,)),
     ]
     in_vmem = pl.BlockSpec(memory_space=pltpu.VMEM)
     return pl.pallas_call(

time: 259 us -> 244 us (0.942)
  Pallas kernels: 258 us -> 242 us
    pallas_call x1, Pallas kernels: 225 us -> 210 us  [step_call(): pl.pallas_call(step_kernel, out_shape=(jax.ShapeDtypeStruct((UNITS * UNIT...]
where the time goes in v4:
time: 244 us; the launch traced here: 243 us
  Pallas kernels  242 us (99%)
    pallas_call x1, Pallas kernels, step_call(): pl.pallas_call(step_kernel, out_shape=(jax.ShapeDtypeStruct((UNITS * UNIT...  210 us
    pallas_call x1, Pallas kernels, adam_call(): pl.pallas_call(adam_kernel, in_specs=[in_vmem, pl.BlockSpec(memory_space=...  32.4 us

profile of v4, /device:TPU:0, one launch (start us, length us, event | category | flops | bytes accessed | tf_op | source)
XLA Modules:
  0.0 243.4 jit_solution(3052719454098815043)
XLA Ops:
  1.3 209.5 %shard_map.425 = (f32[624,384]{1,0:T(8,128)}, f32[224,384]{1,0:T(8,128)}, bf16[768,4096]{1,0:T(8,128)(2,1)}, f32[8,128]{1,0:T(8,128)}) custom-call(bf16[48,3152]{1,0:T(8,128)(2,1)} %bitcast.67, f32[48,384]{1,0:T(8,128)} %refs_0_.1, f32[144,384]{1,0:T(8,128)} %bitcast.59, f32[48,384]{1,0:T(8,128)} %bitcast.63, f32[192,384]{1,0:T(8,128)} %bitcast.51, ...), custom_call_target="tpu_custom_call" | custom-call | flops 49999998976 | bytes 40000000 | tf_op jit(solution)/shard_map/pallas_call | solution.py:1293
  210.8 32.4 %shard_map.426 = (f32[1,1]{1,0:T(1,128)}, f32[1,1]{1,0:T(1,128)}, f32[48,384]{1,0:T(8,128)}, f32[48,384]{1,0:T(8,128)}, f32[48,384]{1,0:T(8,128)}, /*index=5*/f3...) custom-call(f32[8,128]{1,0:T(8,128)} %get-tuple-element.50.scal, ...), custom_call_target="tpu_custom_call" | custom-call | flops 60000000 | bytes 82000000 | tf_op jit(solution)/shard_map/pallas_call | solution.py:1490

commit v5 on v4

--- a/solution.py
+++ b/solution.py
@@ -326,7 +326,7 @@
 UNITS = 13
 BANDS = 8
 G_FIRST = 7
-AHEAD = 4
+AHEAD = 2
 LAG_A = 1
 LAG_B = 3
 LAG_C = 4
@@ -374,13 +374,13 @@
 
 
 def step_kernel(
-    pix_in, patch_in, input_in, output_in, up_in, down_in, tab_in, places, targets, counts, head_in,
-    gout, gtab_out, ghead, scal_out,
+    pix_in, patch_in, input_in, output_in, up_in, down_in, tab_in, places, targets, counts, head_in, drift_in, power_in,
+    gout, gtab_out, ghead, scal_out, head_low, drift_low, power_low,
     wg, px_out, px_mid, px, tb, st0, st1, st2, n1, n2, mix, qkv, hpre, hact,
     hn, hbuf, pk, pkp, pp, lt, pkt, gch, colb, sq, lsb, flip, tmpa, gpk, gps, gpr, g2b, gacc, gst,
     rk, r1a, r1b, r2a, r2b, rz, tab, tabk, tabr, fin,
     ag_send, ag_recv, px_sem, px_send, px_recv, tb_sem, pk_send, pk_recv, ex_send, ex_recv,
-    ls_send, ls_recv, rs_send, rs_recv, tab_send, tab_recv, fin_send, fin_recv, hb_sem, gh_sem, gh_send, gh_recv,
+    ls_send, ls_recv, rs_send, rs_recv, tab_send, tab_recv, fin_send, fin_recv, hb_sem, st_sem, gh_sem, gh_send, gh_recv,
 ):
     r = lax.axis_index("row")
     c = lax.axis_index("col")
@@ -426,10 +426,32 @@
         start += height
     tb[0 : tab_in.shape[0], lanes(r)] = tab_in[...]
     tb[tab_in.shape[0] :, lanes(r)] = jnp.zeros((TOK - tab_in.shape[0], half), wide)
-    hcopy = lambda n: pltpu.make_async_copy(
-        head_in.at[:, pl.ds(pl.multiple_of(n * 256, 256), 256)], hbuf.at[n % 2], hb_sem.at[n % 2]
-    )
-    hcopy(0).start()
+    wide_states = (head_in, drift_in, power_in)
+    low_states = (head_low, drift_low, power_low)
+
+    def state_rows(b):
+        return pl.ds(pl.multiple_of(b * UNIT, UNIT), UNIT)
+
+    def state_in(a, b):
+        return pltpu.make_async_copy(wide_states[a].at[state_rows(b)], hbuf.at[a], hb_sem.at[a])
+
+    wide_part = pkt.shape[1]
+    rest_part = hn.shape[1] - wide_part
+
+    def state_out(a, b):
+        rows = state_rows(b)
+        if a == 0:
+            return [pltpu.make_async_copy(hn.at[rows], head_low.at[rows], st_sem.at[0])]
+        first = pkt.at[UNIT * (a - 1) : UNIT * a]
+        second = pkt.at[UNIT * (a + 1) : UNIT * (a + 2), 0:rest_part]
+        low = low_states[a]
+        return [
+            pltpu.make_async_copy(first, low.at[rows, 0:wide_part], st_sem.at[a]),
+            pltpu.make_async_copy(second, low.at[rows, wide_part:], st_sem.at[a + 2]),
+        ]
+
+    for a in range(3):
+        state_in(a, 0).start()
     pl.semaphore_wait(barrier, 31)
 
     def gather_moves(buf, part, both, send, recv):
@@ -717,14 +739,28 @@
         def _():
             landed(late_moves()[3])
 
-        @pl.when(t < 2 * BANDS)
-        def _():
-            @pl.when(t + 1 < 2 * BANDS)
-            def _():
-                hcopy(t + 1).start()
-
-            hcopy(t).wait()
-            hn[:, pl.ds(pl.multiple_of(t * 256, 256), 256)] = hbuf[t % 2].astype(low_type)
+        @pl.when(t < 16)
+        def _():
+            for a in range(3):
+                state_in(a, t).wait()
+
+                @pl.when(t >= 1)
+                def _():
+                    for copy in state_out(a, t - 1):
+                        copy.wait()
+
+                value = hbuf[a].astype(low_type)
+                if a == 0:
+                    hn[state_rows(t), :] = value
+                else:
+                    pkt[UNIT * (a - 1) : UNIT * a, :] = value[:, :wide_part]
+                    pkt[UNIT * (a + 1) : UNIT * (a + 2), 0:rest_part] = value[:, wide_part:]
+                for copy in state_out(a, t):
+                    copy.start()
+
+                @pl.when(t + 1 < 16)
+                def _():
+                    state_in(a, t + 1).start()
 
         @pl.when(t == LAG_C + 2)
         def _():
@@ -754,6 +790,10 @@
         for moves in weight_moves(n):
             sent(moves)
         return 0
+
+    for a in range(3):
+        for copy in state_out(a, 15):
+            copy.wait()
 
     final_out, _, _ = normed(st2[...], gain(2), shift(2))
     picked = tn(selector.astype(low_type), final_out.astype(low_type)).astype(low_type)
@@ -1230,7 +1270,7 @@
     scal_out[3:8, :] = jnp.zeros((5, 128), wide)
 
 
-def step_call(pix, blocks, tab, places, targets, counts, head):
+def step_call(pix, blocks, tab, places, targets, counts, head, drift, power):
     half = tab.shape[1]
     full = 2 * half
     vocab = head.shape[1]
@@ -1250,7 +1290,7 @@
         vm((4, TOK, full), f32),
         vm((4, TOK, full), b16),
         vm((full, vocab), b16),
-        vm((2, full, 256), f32),
+        vm((3, UNIT, vocab), f32),
         vm((4, 2, 2, 2 * MSLOT, full), b16),
         vm((MSLOT, full), b16),
         vm((2 * MSLOT, full), b16),
@@ -1286,7 +1326,7 @@
         dma((UNITS, 8)), dma((UNITS, 8)),
         dma((6,)), dma((6,)),
         dma((32,)), dma((32,)),
-        dma((2,)),
+        dma((3,)), dma((5,)),
         dma((BANDS // 2,)), dma((BANDS // 2,)), dma((BANDS // 2,)),
     ]
     in_vmem = pl.BlockSpec(memory_space=pltpu.VMEM)
@@ -1297,19 +1337,23 @@
             jax.ShapeDtypeStruct((224, half), f32),
             jax.ShapeDtypeStruct((full, vocab), b16),
             jax.ShapeDtypeStruct((8, 128), f32),
+            *([jax.ShapeDtypeStruct((full, vocab), b16)] * 3),
         ),
         in_specs=[
             *([in_vmem] * 9),
             pl.BlockSpec(memory_space=pltpu.SMEM),
-            pl.BlockSpec(memory_space=pl.ANY),
+            *([pl.BlockSpec(memory_space=pl.ANY)] * 3),
         ],
-        out_specs=(in_vmem, in_vmem, pl.BlockSpec(memory_space=pl.ANY), in_vmem),
+        out_specs=(
+            in_vmem, in_vmem, pl.BlockSpec(memory_space=pl.ANY), in_vmem,
+            *([pl.BlockSpec(memory_space=pl.ANY)] * 3),
+        ),
         scratch_shapes=scratch,
         compiler_params=pltpu.CompilerParams(
             collective_id=0, has_side_effects=True, vmem_limit_bytes=VMEM_LIMIT
         ),
         cost_estimate=pl.CostEstimate(flops=50_000_000_000, bytes_accessed=40_000_000, transcendentals=0),
-    )(pix, *blocks, tab, places, targets, counts, head)
+    )(pix, *blocks, tab, places, targets, counts, head, drift, power)
 
 
 def block_path(
@@ -1322,12 +1366,12 @@
     )
     weights = flat(weights)
     blocks = [weights[n] for n in (0, 2, 3, 4, 5)]
-    gout, gtab, ghead, scal = step_call(
-        pixels.T, blocks, vector_table, mask_places, targets, mask_count, head_weight
-    )
-    results = adam_call(
-        scal, step_count, gout, gtab, ghead, weights, flat(moments[:7]), flat(moments[7:])
-    )
+    drifts, powers = flat(moments[:7]), flat(moments[7:])
+    gout, gtab, ghead, scal, *low = step_call(
+        pixels.T, blocks, vector_table, mask_places, targets, mask_count, head_weight, drifts[6], powers[6]
+    )
+    states = [(*group[:6], value) for group, value in zip((weights, drifts, powers), low)]
+    results = adam_call(scal, step_count, gout, gtab, ghead, *states)
     triples = [results[2 + n :: 3] for n in range(3)]
     triples = [unflat(triple) for triple in triples]
     return (*results[:2], *(triple[n] for n in range(7) for triple in triples))
@@ -1433,8 +1477,7 @@
         def part(q, _):
             at = pl.ds(pl.multiple_of(q * 16, 16), 16)
             values = adam(
-                gbuf[slot, at, :].astype(wide), inbuf[slot, 0, at, :], inbuf[slot, 1, at, :],
-                inbuf[slot, 2, at, :],
+                gbuf[slot, at, :].astype(wide), *(inbuf[slot, m, at, :].astype(wide) for m in range(3))
             )
             for m in range(3):
                 outbuf[spot, m, at, :] = values[m]
@@ -1493,7 +1536,7 @@
         out_specs=[in_vmem] * 2 + [anywhere] * 21,
         out_shape=[one, one] + shapes,
         scratch_shapes=[
-            vm((IN_SLOTS, ROWS, vocab), low_type), vm((IN_SLOTS, 3, ROWS, vocab), wide),
+            vm((IN_SLOTS, ROWS, vocab), low_type), vm((IN_SLOTS, 3, ROWS, vocab), low_type),
             vm((OUT_SLOTS, 3, ROWS, vocab), wide),
             vm((SMALL, half), wide), vm((3, SMALL, half), wide), vm((3, SMALL, half), wide),
             vm(gtab.shape, wide), vm((3, table, half), wide), vm((3, table, half), wide),

time: 244 us -> 231 us (0.947)
  Pallas kernels: 242 us -> 230 us
    pallas_call x1, Pallas kernels: 210 us -> 203 us  [step_call(): pl.pallas_call(step_kernel, out_shape=(jax.ShapeDtypeStruct((UNITS * UNIT...]
    pallas_call x1, Pallas kernels: 32.4 us -> 26.4 us  [adam_call(): pl.pallas_call(adam_kernel, in_specs=[in_vmem, pl.BlockSpec(memory_space=...]
where the time goes in v5:
time: 231 us
  Pallas kernels  230 us (100%)
    pallas_call x1, Pallas kernels, step_call(): pl.pallas_call(step_kernel, out_shape=(jax.ShapeDtypeStruct((UNITS * UNIT...  203 us
    pallas_call x1, Pallas kernels, adam_call(): pl.pallas_call(adam_kernel, in_specs=[in_vmem, pl.BlockSpec(memory_space=...  26.4 us

profile of v5, /device:TPU:0, one launch (start us, length us, event | category | flops | bytes accessed | tf_op | source)
XLA Modules:
  0.0 231.2 jit_solution(12425050900603552668)
XLA Ops:
  1.3 203.3 %shard_map.425 = (f32[624,384]{1,0:T(8,128)}, f32[224,384]{1,0:T(8,128)}, bf16[768,4096]{1,0:T(8,128)(2,1)}, f32[8,128]{1,0:T(8,128)}, bf16[768,4096]{1,0:T(8,12...) custom-call(bf16[48,3152]{1,0:T(8,128)(2,1)} %bitcast.67, f32[48,384]{1,0:T(8,128)} %refs_0_.1, ...), custom_call_target="tpu_custom_call" | custom-call | flops 49999998976 | bytes 40000000 | tf_op jit(solution)/shard_map/pallas_call | solution.py:1333
  204.7 26.4 %shard_map.426 = (f32[1,1]{1,0:T(1,128)}, f32[1,1]{1,0:T(1,128)}, f32[48,384]{1,0:T(8,128)}, f32[48,384]{1,0:T(8,128)}, f32[48,384]{1,0:T(8,128)}, /*index=5*/f3...) custom-call(f32[8,128]{1,0:T(8,128)} %get-tuple-element.53.scal, ...), custom_call_target="tpu_custom_call" | custom-call | flops 60000000 | bytes 82000000 | tf_op jit(solution)/shard_map/pallas_call | solution.py:1533

commit v6 on v5

--- a/solution.py
+++ b/solution.py
@@ -920,11 +920,10 @@
     gps[...] = gpk[other_rows, :].astype(low_type)
     swap_grad = swap(2, gps, gpr, d_y)
     swap_grad.start()
-    picked_third(1)
-    picked_last(0)
     leader = jnp.where(r == 0, 1.0, 0.0)
     loss_part = jnp.sum((log_total * leader - chosen) * weight_col, axis=0, keepdims=True)
     swap_grad.wait()
+    picked_third(1)
     grad_picked = (gpk[own_rows, :] + gpr[...].astype(wide)).astype(low_type)
     grad_final = nn(selector.astype(low_type), grad_picked)
     _, scaled, inverse = normed(st2[...], gain(2), shift(2))
@@ -934,7 +933,6 @@
     gst[4:5, :] = grad_gain
     gst[5:6, :] = grad_shift
     gacc[...] = jnp.zeros_like(gacc)
-    picked_last(1)
 
     def pair_region(n):
         return rk.at[lax.rem(n, 4)]
@@ -1150,7 +1148,7 @@
 
     def back_step(s, _):
         def work(q, _):
-            w = jnp.where(s <= 4, 2 * s - 1 + q, s + 4 + 6 * q)
+            w = jnp.where(s == 0, 15 * q, jnp.where(s <= 4, 2 * s - 1 + q, s + 4 + 6 * q))
 
             @pl.when(jnp.logical_and(w >= 0, w < 4))
             def _():
@@ -1172,18 +1170,18 @@
             def _():
                 back_patch()
 
+            @pl.when(jnp.logical_and(q == 0, s < UNITS))
+            def _():
+                sum_start(sums_moves(s)[0])
+
+            @pl.when(jnp.logical_and(q == 0, jnp.logical_and(s >= 1, s < UNITS + 1)))
+            def _():
+                sums_one(s - 1)
+
             return 0
 
         lax.fori_loop(0, 2, work, 0)
 
-        @pl.when(s < UNITS)
-        def _():
-            sum_start(sums_moves(s)[0])
-
-        @pl.when(jnp.logical_and(s >= 1, s < UNITS + 1))
-        def _():
-            sums_one(s - 1)
-
         @pl.when(jnp.logical_and(s >= 3, s < UNITS + 3))
         def _():
             sums_two(s - 3)
@@ -1196,7 +1194,12 @@
         def _():
             sums_four(s - 7)
 
-        @pl.when(s == 2)
+        for n in range(2):
+            @pl.when(s == n)
+            def _():
+                picked_last(n)
+
+        @pl.when(s == 4)
         def _():
             head_ready()
 

time: 231 us -> 230 us (level)
  no operation moved by 1% of the time
where the time goes in v6:
time: 230 us
  Pallas kernels  229 us (100%)
    pallas_call x1, Pallas kernels, step_call(): pl.pallas_call(step_kernel, out_shape=(jax.ShapeDtypeStruct((UNITS * UNIT...  202 us
    pallas_call x1, Pallas kernels, adam_call(): pl.pallas_call(adam_kernel, in_specs=[in_vmem, pl.BlockSpec(memory_space=...  26.4 us

profile of v6, /device:TPU:0, one launch (start us, length us, event | category | flops | bytes accessed | tf_op | source)
XLA Modules:
  0.0 230.1 jit_solution(92173928306621300)
XLA Ops:
  1.3 202.3 %shard_map.425 = (f32[624,384]{1,0:T(8,128)}, f32[224,384]{1,0:T(8,128)}, bf16[768,4096]{1,0:T(8,128)(2,1)}, f32[8,128]{1,0:T(8,128)}, bf16[768,4096]{1,0:T(8,12...) custom-call(bf16[48,3152]{1,0:T(8,128)(2,1)} %bitcast.67, f32[48,384]{1,0:T(8,128)} %refs_0_.1, ...), custom_call_target="tpu_custom_call" | custom-call | flops 49999998976 | bytes 40000000 | tf_op jit(solution)/shard_map/pallas_call | solution.py:1336
  203.6 26.4 %shard_map.426 = (f32[1,1]{1,0:T(1,128)}, f32[1,1]{1,0:T(1,128)}, f32[48,384]{1,0:T(8,128)}, f32[48,384]{1,0:T(8,128)}, f32[48,384]{1,0:T(8,128)}, /*index=5*/f3...) custom-call(f32[8,128]{1,0:T(8,128)} %get-tuple-element.53.scal, ...), custom_call_target="tpu_custom_call" | custom-call | flops 60000000 | bytes 82000000 | tf_op jit(solution)/shard_map/pallas_call | solution.py:1536

commit v7 on v6

--- a/solution.py
+++ b/solution.py
@@ -1190,9 +1190,9 @@
         def _():
             sums_three(s - 5)
 
-        @pl.when(s >= 7)
-        def _():
-            sums_four(s - 7)
+        @pl.when(s >= 6)
+        def _():
+            sums_four(s - 6)
 
         for n in range(2):
             @pl.when(s == n)
@@ -1224,7 +1224,7 @@
 
         return 0
 
-    lax.fori_loop(0, UNITS + 7, back_step, 0)
+    lax.fori_loop(0, UNITS + 6, back_step, 0)
     gtab_out[rows_own, :] = tab[rows_own, lanes(r)].astype(wide)
     gtab_out[rows_other, :] = tabr[4].astype(wide)
     value = gtab_out[...]

time: 230 us -> 231 us (level)
  no operation moved by 1% of the time
where the time goes in v7:
time: 231 us; the launch traced here: 230 us
  Pallas kernels  229 us (99%)
    pallas_call x1, Pallas kernels, step_call(): pl.pallas_call(step_kernel, out_shape=(jax.ShapeDtypeStruct((UNITS * UNIT...  203 us
    pallas_call x1, Pallas kernels, adam_call(): pl.pallas_call(adam_kernel, in_specs=[in_vmem, pl.BlockSpec(memory_space=...  26.4 us

profile of v7, /device:TPU:0, one launch (start us, length us, event | category | flops | bytes accessed | tf_op | source)
XLA Modules:
  0.0 230.4 jit_solution(2547414945347851383)
XLA Ops:
  1.3 202.5 %shard_map.425 = (f32[624,384]{1,0:T(8,128)}, f32[224,384]{1,0:T(8,128)}, bf16[768,4096]{1,0:T(8,128)(2,1)}, f32[8,128]{1,0:T(8,128)}, bf16[768,4096]{1,0:T(8,12...) custom-call(bf16[48,3152]{1,0:T(8,128)(2,1)} %bitcast.67, f32[48,384]{1,0:T(8,128)} %refs_0_.1, ...), custom_call_target="tpu_custom_call" | custom-call | flops 49999998976 | bytes 40000000 | tf_op jit(solution)/shard_map/pallas_call | solution.py:1336
  203.9 26.4 %shard_map.426 = (f32[1,1]{1,0:T(1,128)}, f32[1,1]{1,0:T(1,128)}, f32[48,384]{1,0:T(8,128)}, f32[48,384]{1,0:T(8,128)}, f32[48,384]{1,0:T(8,128)}, /*index=5*/f3...) custom-call(f32[8,128]{1,0:T(8,128)} %get-tuple-element.53.scal, ...), custom_call_target="tpu_custom_call" | custom-call | flops 60000000 | bytes 82000000 | tf_op jit(solution)/shard_map/pallas_call | solution.py:1536
